TPU v7x, 32 devices: a whole 2x2x4 slice. The times are simulated.
32 devices in a mesh: expert: 8 (over z, core), dp: 4 (over y, x).
Axes of the slice: x: 2, y: 2, z: 4, core: 2. Of those that a mesh axis runs over, the one named last changes fastest.
Arguments:
- tokens: bfloat16 [4096, 3584], P(('expert', 'dp')), may hold values from -6 to 6
- expert_ids: int32 [4096, 8], P(('expert', 'dp')), may hold values from 0 to 63, all different within a row
- gate_probs: float32 [4096, 8], P(('expert', 'dp')), may hold values from 0.02 to 0.5
- out_grad: bfloat16 [4096, 3584], P(('expert', 'dp')), may hold values from -6 to 6
- w_gate: bfloat16 [8, 1024, 3584], P('expert', 'dp'), may hold values from -0.09375 to 0.09375
- w_up: bfloat16 [8, 1024, 3584], P('expert', 'dp'), may hold values from -0.09375 to 0.09375
- w_down: bfloat16 [8, 1024, 3584], P('expert', 'dp'), may hold values from -0.1875 to 0.1875
Outputs:
- grad_gate: bfloat16 [8, 1024, 3584], P('expert', 'dp')
- grad_up: bfloat16 [8, 1024, 3584], P('expert', 'dp')
- grad_down: bfloat16 [8, 1024, 3584], P('expert', 'dp')
All inputs are finite; a program needn't handle non-finite values.
Results may differ from a plain program's by a relative error of at most 0.0058.
Values may be sent and summed in bfloat16 or wider, within the bound.
No kernel may reach another device: no remote copies, remote signals or barrier semaphores. Data moves between devices by JAX's collectives and lax.ppermute only.
A program may use at most 64 MiB of HBM per device.

v0:
```python
import jax
import jax.numpy as jnp
from jax import lax
from jax.sharding import PartitionSpec as P

CAP = 2


def local_factors(rows_x, rows_dy, weight_gate, weight_up, weight_down):
    contract = (((1,), (1,)), ((), ()))
    gate_pre = lax.dot_general(rows_x, weight_gate, contract, preferred_element_type=jnp.float32)
    up_pre = lax.dot_general(rows_x, weight_up, contract, preferred_element_type=jnp.float32)
    back_grad = lax.dot_general(rows_dy, weight_down, contract, preferred_element_type=jnp.float32)
    sig_gate = jax.nn.sigmoid(gate_pre)
    act_gate = gate_pre * sig_gate
    hidden = (act_gate * up_pre).astype(jnp.bfloat16)
    d_gate = (back_grad * up_pre * sig_gate * (1.0 + gate_pre * (1.0 - sig_gate))).astype(
        jnp.bfloat16
    )
    d_up = (back_grad * act_gate).astype(jnp.bfloat16)
    return (d_gate, d_up, hidden)


def outer_sum(factor, rows):
    return lax.dot_general(
        factor, rows, (((0,), (0,)), ((), ())), preferred_element_type=jnp.float32
    )


def local(tokens, expert_ids, gate_probs, out_grad, w_gate, w_up, w_down):
    n_expert = lax.axis_size("expert")
    experts_all = w_gate.shape[0] * n_expert
    tok_rows, top_count = expert_ids.shape
    feature_count = tokens.shape[1]
    flat_ids = expert_ids.reshape(-1)
    expert_range = jnp.arange(experts_all, dtype=jnp.int32)
    onehot = (flat_ids[:, None] == expert_range[None, :]).astype(jnp.int32)
    before = jnp.cumsum(onehot, axis=0) - onehot
    slot_rank = jnp.sum(before * onehot, axis=1)
    kept_mask = (flat_ids < experts_all) & (slot_rank < CAP)
    slot_index = jnp.where(kept_mask, flat_ids * CAP + slot_rank, -1)
    slot_range = jnp.arange(experts_all * CAP, dtype=jnp.int32)
    matches = (slot_index[None, :] == slot_range[:, None]).astype(jnp.float32)
    matches = matches.reshape(experts_all * CAP, tok_rows, top_count)
    picker = jnp.sum(matches, axis=2).astype(jnp.bfloat16)
    slot_prob = jnp.sum(matches * gate_probs[None, :, :], axis=(1, 2))
    sent_x = jnp.dot(picker, tokens, preferred_element_type=jnp.float32).astype(jnp.bfloat16)
    sent_dy = (
        jnp.dot(picker, out_grad, preferred_element_type=jnp.float32) * slot_prob[:, None]
    ).astype(jnp.bfloat16)
    sent_x = sent_x.reshape(experts_all, CAP, feature_count)
    sent_dy = sent_dy.reshape(experts_all, CAP, feature_count)
    recv_x, recv_dy = (
        lax.all_to_all(sent_x, "expert", split_axis=0, concat_axis=0, tiled=True),
        lax.all_to_all(sent_dy, "expert", split_axis=0, concat_axis=0, tiled=True),
    )
    rows_x = recv_x.reshape(-1, feature_count)
    rows_dy = recv_dy.reshape(-1, feature_count)
    piece_x = lax.all_gather(rows_x, "dp", axis=0, tiled=True)
    piece_dy = lax.all_gather(rows_dy, "dp", axis=0, tiled=True)
    d_gate, d_up, hidden = local_factors(piece_x, piece_dy, w_gate[0], w_up[0], w_down[0])
    term_gate = outer_sum(d_gate, piece_x)
    term_up = outer_sum(d_up, piece_x)
    term_down = outer_sum(hidden, piece_dy)
    return (
        term_gate.astype(jnp.bfloat16)[None],
        term_up.astype(jnp.bfloat16)[None],
        term_down.astype(jnp.bfloat16)[None],
    )


def solution(mesh):
    in_specs = (
        P(("expert", "dp"), None),
        P(("expert", "dp"), None),
        P(("expert", "dp"), None),
        P(("expert", "dp"), None),
        P("expert", "dp", None),
        P("expert", "dp", None),
        P("expert", "dp", None),
    )
    out_specs = (P("expert", "dp", None), P("expert", "dp", None), P("expert", "dp", None))
    return jax.shard_map(local, mesh=mesh, in_specs=in_specs, out_specs=out_specs, check_vma=False)
```

profile of v0, /device:TPU:0, one launch (start us, length us, event | category | flops | bytes accessed | tf_op | source)
XLA Modules:
  0.0 54.7 jit_solution(2732195532551741704)
XLA Ops:
  0.6 0.0 copy-start
  0.6 0.0 copy-start.2
  0.7 0.9 %copy.26 = s32[128,8]{1,0:T(8,128)S(1)} copy(s32[128,8]{0,1:T(8,128)} %param.8) | data formatting | bytes 8192 | tf_op args[1]
  1.6 0.1 eq.43
  1.7 0.1 eq.39
  1.8 2.3 %reduce-window.6 = s32[8,8,128]{2,1,0:T(8,128)S(1)} reduce-window(s32[8,8,128]{2,1,0:T(8,128)S(1)} %fusion.15, s32[]{:T(128)} %constant.4.clone.1), window={size=1x1x128 pad=0_0x0_0x127_0}, to_apply=%region_0.0 | reduce-window | flops 1040384 | bytes 65540 | tf_op jit(solution)/shard_map/reduce-window
  4.1 0.3 slice_reduce_fusion
  4.3 0.2 reduce-window.9
  4.5 0.1 add_bitcast_fusion
  4.6 0.1 reduce_sum.30
  4.8 0.7 %add_select_fusion = s32[128,8]{0,1:T(8,128)S(1)} fusion(s32[128,8]{0,1:T(8,128)S(1)} %copy.28, s32[128,8]{0,1:T(8,128)} %param.8), kind=kLoop, calls=%fused_computation.33 | loop fusion | flops 6144 | bytes 12288 | tf_op jit(solution)/shard_map/jit(_where)/select_n | solution.py:41
  5.5 0.9 %select_reduce_fusion = (f32[16]{0:T(128)S(1)}, bf16[16,128]{1,0:T(8,128)(2,1)S(1)}) fusion(f32[128,8]{0,1:T(8,128)} %param.9, s32[128,8]{0,1:T(8,128)S(1)} %add_select_fusion), kind=kLoop, calls=%fused_computation.20 | loop fusion | flops 79856 | bytes 12352 | tf_op jit(solution)/shard_map/reduce_sum | solution.py:46
  6.4 1.4 %convolution_convert_fusion.3 = bf16[16,3584]{1,0:T(8,128)(2,1)S(1)} fusion(bf16[128,3584]{1,0:T(8,128)(2,1)} %param.7, bf16[16,128]{1,0:T(8,128)(2,1)S(1)} %get-tuple-element.4), kind=kOutput, calls=%fused_computation.8 | convolution fusion | flops 14737408 | bytes 1036288 | tf_op jit(solution)/shard_map/dot_general | solution.py:47
  7.8 0.7 %reshape.64 = bf16[8,2,3584]{2,1,0:T(2,128)(2,1)} reshape(bf16[16,3584]{1,0:T(8,128)(2,1)S(1)} %convolution_convert_fusion.3) | data formatting | bytes 229376 | tf_op jit(solution)/shard_map/reshape | solution.py:51
  8.5 6.3 %all-to-all-start.1 = ((bf16[8,2,3584]{2,1,0:T(2,128)(2,1)}), bf16[8,2,3584]{2,1,0:T(2,128)(2,1)S(1)}, u32[]{:S(2)}, u32[]{:S(2)}) async-start(bf16[8,2,3584]{2,1,0:T(2,128)(2,1)} %reshape.64), calls=%async_computation.1 | async-start | bytes 229376 | tf_op jit(solution)/shard_map/all_to_all | solution.py:54
  14.8 0.0 copy-done.2
  14.8 0.2 fusion.3
  15.0 0.7 %reshape.62 = bf16[8,2,3584]{2,1,0:T(2,128)(2,1)} reshape(bf16[16,3584]{1,0:T(8,128)(2,1)S(1)} %fusion.3) | data formatting | bytes 229376 | tf_op jit(solution)/shard_map/reshape | solution.py:52
  15.7 5.6 %all-to-all-done.1 = bf16[8,2,3584]{2,1,0:T(2,128)(2,1)S(1)} async-done(((bf16[8,2,3584]{2,1,0:T(2,128)(2,1)}), bf16[8,2,3584]{2,1,0:T(2,128)(2,1)S(1)}, u32[]{:S(2)}, u32[]{:S(2)}) %all-to-all-start.1) | async-done | bytes 114720 | tf_op jit(solution)/shard_map/all_to_all | solution.py:54
  21.4 3.4 %all-to-all-start = ((bf16[8,2,3584]{2,1,0:T(2,128)(2,1)}), bf16[8,2,3584]{2,1,0:T(2,128)(2,1)S(1)}, u32[]{:S(2)}, u32[]{:S(2)}) async-start(bf16[8,2,3584]{2,1,0:T(2,128)(2,1)} %reshape.62), calls=%async_computation | async-start | bytes 229376 | tf_op jit(solution)/shard_map/all_to_all | solution.py:55
  24.8 0.0 copy-start.1
  24.8 10.2 %all_gather.7 = bf16[64,3584]{1,0:T(8,128)(2,1)S(1)} all-gather(bf16[16,3584]{1,0:T(8,128)(2,1)S(1)} %reshape.65), channel_id=1, replica_groups=mesh['expert'=8,'dp'=4] {'dp'}, dimensions={0}, use_global_device_ids=true | all-gather | bytes 573440 | tf_op jit(solution)/shard_map/all_gather | solution.py:59
  35.0 0.0 copy-done
  35.0 0.7 %fusion.4 = f32[64,256]{1,0:T(8,128)S(1)} fusion(bf16[64,3584]{1,0:T(8,128)(2,1)S(1)} %all_gather.7, bf16[1,256,3584]{2,1,0:T(8,128)(2,1)S(1)} %copy-done), kind=kOutput, calls=%fused_computation.9 | convolution fusion | flops 117440512 | bytes 2359296 | tf_op jit(solution)/shard_map/dot_general | solution.py:11
  35.7 0.0 copy-done.1
  35.7 0.7 %fusion.6 = f32[64,256]{1,0:T(8,128)S(1)} fusion(bf16[64,3584]{1,0:T(8,128)(2,1)S(1)} %all_gather.7, bf16[1,256,3584]{2,1,0:T(8,128)(2,1)S(1)} %copy-done.1), kind=kOutput, calls=%fused_computation.11 | convolution fusion | flops 117440512 | bytes 2359296 | tf_op jit(solution)/shard_map/dot_general | solution.py:12
  36.3 0.0 all-to-all-done
  36.4 10.4 %all_gather.6 = bf16[64,3584]{1,0:T(8,128)(2,1)S(1)} all-gather(bf16[16,3584]{1,0:T(8,128)(2,1)S(1)} %reshape.63), channel_id=1, replica_groups=mesh['expert'=8,'dp'=4] {'dp'}, dimensions={0}, use_global_device_ids=true | all-gather | bytes 573440 | tf_op jit(solution)/shard_map/all_gather | solution.py:60
  46.8 2.2 %fusion.8 = f32[64,256]{1,0:T(8,128)S(1)} fusion(bf16[64,3584]{1,0:T(8,128)(2,1)S(1)} %all_gather.6, bf16[1,256,3584]{2,1,0:T(8,128)(2,1)} %param.13), kind=kOutput, calls=%fused_computation.13 | convolution fusion | flops 117440512 | bytes 2359296 | tf_op jit(solution)/shard_map/dot_general | solution.py:13
  48.9 1.9 %fusion.2 = bf16[1,256,3584]{2,1,0:T(8,128)(2,1)} fusion(bf16[64,3584]{1,0:T(8,128)(2,1)S(1)} %all_gather.6, f32[64,256]{1,0:T(8,128)S(1)} %fusion.6, f32[64,256]{1,0:T(8,128)S(1)} %fusion.4), kind=kOutput, calls=%fused_computation.5 | convolution fusion | flops 118456320 | bytes 2424832 | tf_op jit(solution)/shard_map/dot_general | solution.py:25
  50.9 1.9 %fusion = bf16[1,256,3584]{2,1,0:T(8,128)(2,1)} fusion(bf16[64,3584]{1,0:T(8,128)(2,1)S(1)} %all_gather.7, f32[64,256]{1,0:T(8,128)S(1)} %fusion.4, f32[64,256]{1,0:T(8,128)S(1)} %fusion.8, f32[64,256]{1,0:T(8,128)S(1)} %fusion.6), kind=kOutput, calls=%fused_computation.3 | convolution fusion | flops 118521856 | bytes 2490368 | tf_op jit(solution)/shard_map/dot_general | solution.py:25
  52.8 1.9 %fusion.1 = bf16[1,256,3584]{2,1,0:T(8,128)(2,1)} fusion(bf16[64,3584]{1,0:T(8,128)(2,1)S(1)} %all_gather.7, f32[64,256]{1,0:T(8,128)S(1)} %fusion.8, f32[64,256]{1,0:T(8,128)S(1)} %fusion.4), kind=kOutput, calls=%fused_computation.4 | convolution fusion | flops 118456320 | bytes 2424832 | tf_op jit(solution)/shard_map/dot_general | solution.py:25
  (5 shorter events, 0.2 us)
Async XLA Ops:
  0.6 34.4 %copy-start = (bf16[1,256,3584]{2,1,0:T(8,128)(2,1)S(1)}, bf16[1,256,3584]{2,1,0:T(8,128)(2,1)}, u32[]{:S(2)}) copy-start(bf16[1,256,3584]{2,1,0:T(8,128)(2,1)} %param.11) | copy-start | bytes 5505028
  0.6 14.2 %copy-start.2 = (bf16[128,3584]{1,0:T(8,128)(2,1)S(1)}, bf16[128,3584]{1,0:T(8,128)(2,1)}, u32[]{:S(2)}) copy-start(bf16[128,3584]{1,0:T(8,128)(2,1)} %param.10) | copy-start | bytes 2752516
  8.5 12.9 %all-to-all-start.1 = ((bf16[8,2,3584]{2,1,0:T(2,128)(2,1)}), bf16[8,2,3584]{2,1,0:T(2,128)(2,1)S(1)}, u32[]{:S(2)}, u32[]{:S(2)}) async-start(bf16[8,2,3584]{2,1,0:T(2,128)(2,1)} %reshape.64), calls=%async_computation.1 | async-start | bytes 229376 | tf_op jit(solution)/shard_map/all_to_all | solution.py:54
  21.4 15.0 %all-to-all-start = ((bf16[8,2,3584]{2,1,0:T(2,128)(2,1)}), bf16[8,2,3584]{2,1,0:T(2,128)(2,1)S(1)}, u32[]{:S(2)}, u32[]{:S(2)}) async-start(bf16[8,2,3584]{2,1,0:T(2,128)(2,1)} %reshape.62), calls=%async_computation | async-start | bytes 229376 | tf_op jit(solution)/shard_map/all_to_all | solution.py:55
  24.8 10.9 %copy-start.1 = (bf16[1,256,3584]{2,1,0:T(8,128)(2,1)S(1)}, bf16[1,256,3584]{2,1,0:T(8,128)(2,1)}, u32[]{:S(2)}) copy-start(bf16[1,256,3584]{2,1,0:T(8,128)(2,1)} %param.12) | copy-start | bytes 5505028
where the time goes:
time: 55.2 us; the launch traced here: 54.7 us
  blocking collectives  20.6 us (37%)
  matrix products  10.8 us (20%)
  starting transfers between devices  9.69 us (18%)
  waiting for transfers between devices  5.63 us (10%)
  other arithmetic  4.14 us (7%)
  local copies, waits for them, and re-layouts  3.05 us (6%)
  between operations  0.75 us (1%)
    all_gather x1, blocking collectives, local(): piece_dy = lax.all_gather(rows_dy, 'dp', axis=0, tiled=True)  10.4 us
    all_gather x1, blocking collectives, local(): piece_x = lax.all_gather(rows_x, 'dp', axis=0, tiled=True)  10.2 us
    all_to_all x1, starting transfers between devices, local(): lax.all_to_all(sent_x, 'expert', split_axis=0, concat_axis=0, tiled=True)  6.33 us
    dot_general x3, matrix products, outer_sum(): lax.dot_general(factor, rows, (((0,), (0,)), ((), ())), preferred_element...  5.71 us
    all_to_all x1, waiting for transfers between devices, local(): lax.all_to_all(sent_x, 'expert', split_axis=0, concat_axis=0, tiled=True)  5.62 us
    all_to_all x1, starting transfers between devices, local(): lax.all_to_all(sent_dy, 'expert', split_axis=0, concat_axis=0, tiled=True)  3.37 us
    another operation x2, other arithmetic  2.43 us
    dot_general x1, matrix products, local_factors(): lax.dot_general(rows_dy, weight_down, contract, preferred_element_type=jn...  2.16 us
  transfers between devices with their start and end apart: 2, of which 1 were waited for; matrix products, arithmetic and copies ran while one was open for 4% of the time, Pallas kernels for 0%

commit v1 on v0

v1 whole, which is shorter than its diff:
```python
import functools

import jax
import jax.numpy as jnp
from jax import lax
from jax.experimental import pallas as pl
from jax.experimental.pallas import tpu as pltpu
from jax.sharding import PartitionSpec as P

CAP = 2


def pick_kernel(experts, order_ref, ids_ref, probs_ref, tokens_hbm, grad_hbm, out_ref, tok_buf, grad_buf, sems):
    pieces = sems.shape[1]
    width = tok_buf.shape[1] // pieces
    copies = []
    for part in range(pieces):
        cols = pl.ds(part * width, width)
        copies.append(
            (
                pltpu.make_async_copy(tokens_hbm.at[:, cols], tok_buf.at[:, cols], sems.at[0, part]),
                pltpu.make_async_copy(grad_hbm.at[:, cols], grad_buf.at[:, cols], sems.at[1, part]),
            )
        )
    for copy_x, copy_dy in copies:
        copy_x.start()
        copy_dy.start()
    top, count = ids_ref.shape
    order = order_ref[...]
    named = jnp.zeros((experts, count), jnp.float32)
    prob = jnp.zeros((experts, count), jnp.float32)
    for k in range(top):
        hit = ids_ref[k : k + 1, :] == order
        named = jnp.where(hit, 1.0, named)
        prob = jnp.where(hit, probs_ref[k : k + 1, :], prob)
    earlier = (
        lax.broadcasted_iota(jnp.int32, (count, count), 0)
        < lax.broadcasted_iota(jnp.int32, (count, count), 1)
    ).astype(jnp.bfloat16)
    rank = jnp.dot(named.astype(jnp.bfloat16), earlier, preferred_element_type=jnp.float32)
    pickers = []
    for slot in range(CAP):
        pickers.append(jnp.where((named > 0.5) & (rank == float(slot)), 1.0, 0.0))
    weights = [jnp.sum(picker * prob, axis=1, keepdims=True) for picker in pickers]
    picker = jnp.stack(pickers, axis=1).reshape(experts * CAP, count).astype(jnp.bfloat16)
    weight = jnp.stack(weights, axis=1).reshape(experts * CAP, 1)
    for part in range(pieces):
        cols = pl.ds(part * width, width)
        copy_x, copy_dy = copies[part]
        copy_x.wait()
        rows_x = jnp.dot(picker, tok_buf[:, cols], preferred_element_type=jnp.float32)
        out_ref[:, 0:CAP, cols] = rows_x.reshape(experts, CAP, width).astype(jnp.bfloat16)
        copy_dy.wait()
        rows_dy = jnp.dot(picker, grad_buf[:, cols], preferred_element_type=jnp.float32) * weight
        out_ref[:, CAP : 2 * CAP, cols] = rows_dy.reshape(experts, CAP, width).astype(jnp.bfloat16)


def pick_rows(order, ids, probs, tokens, out_grad):
    experts = order.shape[0]
    count, channels = tokens.shape
    pieces = 4
    vmem = pl.BlockSpec(memory_space=pltpu.VMEM)
    hbm = pl.BlockSpec(memory_space=pltpu.HBM)
    return pl.pallas_call(
        functools.partial(pick_kernel, experts),
        out_shape=jax.ShapeDtypeStruct((experts, 2 * CAP, channels), jnp.bfloat16),
        in_specs=[vmem, vmem, vmem, hbm, hbm],
        out_specs=vmem,
        scratch_shapes=[
            pltpu.VMEM((count, channels), jnp.bfloat16),
            pltpu.VMEM((count, channels), jnp.bfloat16),
            pltpu.SemaphoreType.DMA((2, pieces)),
        ],
        compiler_params=pltpu.CompilerParams(vmem_limit_bytes=16 * 1024 * 1024),
    )(order, ids, probs, tokens, out_grad)


def grads_kernel(rows_ref, gate_ref, up_ref, down_ref, out_gate, out_up, out_down, buf, sems):
    rows = rows_ref[...]
    count, channels = rows.shape
    contract = (((1,), (1,)), ((), ()))
    gate_pre = lax.dot_general(rows, gate_ref[...], contract, preferred_element_type=jnp.float32)
    up_pre = lax.dot_general(rows, up_ref[...], contract, preferred_element_type=jnp.float32)
    back_grad = lax.dot_general(rows, down_ref[...], contract, preferred_element_type=jnp.float32)
    back_grad = pltpu.roll(back_grad, count - CAP, 0)
    is_x = lax.broadcasted_iota(jnp.int32, (count, 1), 0) % (2 * CAP) < CAP
    sig_gate = jax.nn.sigmoid(gate_pre)
    act_gate = gate_pre * sig_gate
    hidden = jnp.where(is_x, act_gate * up_pre, 0.0)
    d_gate = jnp.where(is_x, back_grad * up_pre * sig_gate * (1.0 + gate_pre * (1.0 - sig_gate)), 0.0)
    d_up = jnp.where(is_x, back_grad * act_gate, 0.0)
    hidden = pltpu.roll(hidden, CAP, 0)
    pieces = sems.shape[1]
    width = channels // pieces
    copies = []
    for number, (factor, out) in enumerate(((hidden, out_down), (d_up, out_up), (d_gate, out_gate))):
        turned = factor.T.astype(jnp.bfloat16)
        for part in range(pieces):
            cols = pl.ds(part * width, width)
            term = jnp.dot(turned, rows_ref[:, cols], preferred_element_type=jnp.float32)
            buf[number, :, cols] = term.astype(jnp.bfloat16)
            copy = pltpu.make_async_copy(buf.at[number, :, cols], out.at[:, cols], sems.at[number, part])
            copy.start()
            copies.append(copy)
    for copy in copies:
        copy.wait()


def weight_grads(rows, w_gate, w_up, w_down):
    units, channels = w_gate.shape
    pieces = 4
    vmem = pl.BlockSpec(memory_space=pltpu.VMEM)
    hbm = pl.BlockSpec(memory_space=pltpu.HBM)
    shape = jax.ShapeDtypeStruct((units, channels), jnp.bfloat16)
    return pl.pallas_call(
        grads_kernel,
        out_shape=(shape, shape, shape),
        in_specs=[vmem] * 4,
        out_specs=(hbm, hbm, hbm),
        scratch_shapes=[
            pltpu.VMEM((3, units, channels), jnp.bfloat16),
            pltpu.SemaphoreType.DMA((3, pieces)),
        ],
        compiler_params=pltpu.CompilerParams(vmem_limit_bytes=20 * 1024 * 1024),
    )(rows, w_gate, w_up, w_down)


def local(tokens, expert_ids, gate_probs, out_grad, w_gate, w_up, w_down):
    n_expert = lax.axis_size("expert")
    experts_all = w_gate.shape[0] * n_expert
    channels = tokens.shape[1]
    order = jnp.arange(experts_all, dtype=jnp.int32)[:, None]
    sent = pick_rows(order, expert_ids.T, gate_probs.T, tokens, out_grad)
    recv = lax.all_to_all(sent, "expert", split_axis=0, concat_axis=0, tiled=True)
    rows = lax.all_gather(recv.reshape(-1, channels), "dp", axis=0, tiled=True)
    grads = weight_grads(rows, w_gate[0], w_up[0], w_down[0])
    return tuple(grad[None] for grad in grads)


def solution(mesh):
    in_specs = (
        P(("expert", "dp"), None),
        P(("expert", "dp"), None),
        P(("expert", "dp"), None),
        P(("expert", "dp"), None),
        P("expert", "dp", None),
        P("expert", "dp", None),
        P("expert", "dp", None),
    )
    out_specs = (P("expert", "dp", None), P("expert", "dp", None), P("expert", "dp", None))
    return jax.shard_map(local, mesh=mesh, in_specs=in_specs, out_specs=out_specs, check_vma=False)
```

time: 55.2 us -> 41.4 us (0.75)
  matrix products: 10.8 us -> 0 us
  starting transfers between devices: 9.69 us -> 0 us
  blocking collectives: 20.6 us -> 27.2 us
  Pallas kernels: 0 us -> 6.41 us
  waiting for transfers between devices: 5.63 us -> 0 us
  other arithmetic: 4.14 us -> 0 us
  local copies, waits for them, and re-layouts: 3.05 us -> 6.78 us
    all_to_all x0 -> x1, blocking collectives: none -> 15.2 us  [local(): lax.all_to_all(sent, 'expert', split_axis=0, concat_axis=0, tiled=True)]
    dot_general x8 -> x0, matrix products: 10.8 us -> none  [the longest x3 5.71 us: outer_sum(): lax.dot_general(factor, rows, (((0,), (0,)), ((), ())), preferred_element...]
    all_to_all x2 -> x0, starting transfers between devices: 9.69 us -> none  [the longest x1 6.33 us: local(): lax.all_to_all(sent_x, 'expert', split_axis=0, concat_axis=0, tiled=True)]
    all_gather x2 -> x1, blocking collectives: 20.6 us -> 12 us  [local(): rows = lax.all_gather(recv.reshape(-1, channels), 'dp', axis=0, tiled=True)]
    pallas_call x0 -> x2, Pallas kernels: none -> 6.41 us  [the longest x1 4.57 us: weight_grads(): pl.pallas_call(grads_kernel, out_shape=(shape, shape, shape), in_specs=[v...]
    unnamed x7 -> x14, local copies, waits for them, and re-layouts: 0.96 us -> 6.72 us
    all_to_all x2 -> x0, waiting for transfers between devices: 5.63 us -> none  [the longest x1 5.62 us: local(): lax.all_to_all(sent_x, 'expert', split_axis=0, concat_axis=0, tiled=True)]
    another operation x2 -> x0, other arithmetic: 2.43 us -> none
  transfers between devices with their start and end apart: 2 -> 0, of which waited for: 1 -> 0; matrix products, arithmetic and copies ran while one was open for 4% -> 0% of each run, Pallas kernels for 0% -> 0%
where the time goes in v1:
time: 41.4 us; the launch traced here: 41 us
  blocking collectives  27.2 us (66%)
  local copies, waits for them, and re-layouts  6.78 us (16%)
  Pallas kernels  6.41 us (15%)
  between operations  0.67 us (2%)
    all_to_all x1, blocking collectives, local(): lax.all_to_all(sent, 'expert', split_axis=0, concat_axis=0, tiled=True)  15.2 us
    all_gather x1, blocking collectives, local(): rows = lax.all_gather(recv.reshape(-1, channels), 'dp', axis=0, tiled=True)  12 us
    unnamed x14, local copies, waits for them, and re-layouts  6.72 us
    pallas_call x1, Pallas kernels, weight_grads(): pl.pallas_call(grads_kernel, out_shape=(shape, shape, shape), in_specs=[v...  4.57 us
    pallas_call x1, Pallas kernels, pick_rows(): pl.pallas_call(functools.partial(pick_kernel, experts), out_shape=jax.Sha...  1.84 us

profile of v1, /device:TPU:0, one launch (start us, length us, event | category | flops | bytes accessed | tf_op | source)
XLA Modules:
  0.0 41.0 jit_solution(6516264363945618296)
XLA Ops:
  0.6 0.0 copy-start.3
  0.7 1.2 %copy-done.3 = bf16[128,3584]{1,0:T(8,128)(2,1)S(1)} copy-done((bf16[128,3584]{1,0:T(8,128)(2,1)S(1)}, bf16[128,3584]{1,0:T(8,128)(2,1)}, u32[]{:S(2)}) %copy-start.3) | copy-done | bytes 917528
  1.8 0.0 copy-start.4
  1.8 1.2 %copy-done.4 = bf16[128,3584]{1,0:T(8,128)(2,1)S(1)} copy-done((bf16[128,3584]{1,0:T(8,128)(2,1)S(1)}, bf16[128,3584]{1,0:T(8,128)(2,1)}, u32[]{:S(2)}) %copy-start.4) | copy-done | bytes 917528
  3.0 0.0 copy-start.5
  3.0 0.7 %copy-done.5 = s32[128,8]{0,1:T(8,128)S(1)} copy-done((s32[128,8]{0,1:T(8,128)S(1)}, s32[128,8]{0,1:T(8,128)}, u32[]{:S(2)}) %copy-start.5) | copy-done | bytes 4120
  3.7 0.0 copy-start.6
  3.7 0.7 %copy-done.6 = f32[128,8]{0,1:T(8,128)S(1)} copy-done((f32[128,8]{0,1:T(8,128)S(1)}, f32[128,8]{0,1:T(8,128)}, u32[]{:S(2)}) %copy-start.6) | copy-done | bytes 4120
  4.4 0.0 copy-start
  4.4 1.8 %shard_map.94 = bf16[8,4,3584]{2,1,0:T(4,128)(2,1)S(1)} custom-call(s32[8,1]{1,0:T(8,128)S(1)} %iota.4.order_ref, s32[8,128]{1,0:T(8,128)S(1)} %bitcast.11, f32[8,128]{1,0:T(8,128)S(1)} %bitcast.12, bf16[128,3584]{1,0:T(8,128)(2,1)S(1)} %copy-done.3, bf16[128,3584]{1,0:T(8,128)(2,1)S(1)} %copy-done.4), custom_call_target="tpu_custom_call" | custom-call | tf_op jit(solution)/shard_map/pallas_call | solution.py:64
  6.2 15.2 %all_to_all.5 = bf16[8,4,3584]{2,1,0:T(4,128)(2,1)S(1)} all-to-all(bf16[8,4,3584]{2,1,0:T(4,128)(2,1)S(1)} %shard_map.94), channel_id=1, replica_groups=mesh['expert'=8,'dp'=4] {'expert'}, dimensions={0} | all-to-all | bytes 458752 | tf_op jit(solution)/shard_map/all_to_all | solution.py:134
  21.4 0.1 reshape.9
  21.5 12.0 %all_gather.3.rows_ref = bf16[128,3584]{1,0:T(8,128)(2,1)S(1)} all-gather(bf16[32,3584]{1,0:T(8,128)(2,1)S(1)} %reshape.9), channel_id=1, replica_groups=mesh['expert'=8,'dp'=4] {'dp'}, dimensions={0}, use_global_device_ids=true | all-gather | bytes 1146880 | tf_op jit(solution)/shard_map/all_gather | solution.py:135
  33.5 0.0 copy-done
  33.5 0.0 copy-start.1
  33.5 1.5 %copy-done.1 = bf16[1,256,3584]{2,1,0:T(8,128)(2,1)S(1)} copy-done((bf16[1,256,3584]{2,1,0:T(8,128)(2,1)S(1)}, bf16[1,256,3584]{2,1,0:T(8,128)(2,1)}, u32[]{:S(2)}) %copy-start.1) | copy-done | bytes 1835032
  35.0 0.0 copy-start.2
  35.0 1.5 %copy-done.2 = bf16[1,256,3584]{2,1,0:T(8,128)(2,1)S(1)} copy-done((bf16[1,256,3584]{2,1,0:T(8,128)(2,1)S(1)}, bf16[1,256,3584]{2,1,0:T(8,128)(2,1)}, u32[]{:S(2)}) %copy-start.2) | copy-done | bytes 1835032
  36.5 4.6 %shard_map.95 = (bf16[256,3584]{1,0:T(8,128)(2,1)}, bf16[256,3584]{1,0:T(8,128)(2,1)}, bf16[256,3584]{1,0:T(8,128)(2,1)}) custom-call(bf16[128,3584]{1,0:T(8,128)(2,1)S(1)} %all_gather.3.rows_ref, bf16[256,3584]{1,0:T(8,128)(2,1)S(1)} %bitcast.8, bf16[256,3584]{1,0:T(8,128)(2,1)S(1)} %bitcast.9, bf16[256,3584]{1,0:T(8,128)(2,1)S(1)} %bitcast.10), custom_call_target="tpu_custom_call" | custom-call | tf_op jit(solution)/shard_map/pallas_call | solution.py:115
  (1 shorter events, 0.0 us)
Async XLA Ops:
  0.6 1.2 %copy-start.3 = (bf16[128,3584]{1,0:T(8,128)(2,1)S(1)}, bf16[128,3584]{1,0:T(8,128)(2,1)}, u32[]{:S(2)}) copy-start(bf16[128,3584]{1,0:T(8,128)(2,1)} %tokens_hbm.1) | copy-start | bytes 2752516
  1.8 1.2 %copy-start.4 = (bf16[128,3584]{1,0:T(8,128)(2,1)S(1)}, bf16[128,3584]{1,0:T(8,128)(2,1)}, u32[]{:S(2)}) copy-start(bf16[128,3584]{1,0:T(8,128)(2,1)} %grad_hbm.1) | copy-start | bytes 2752516
  3.0 0.7 %copy-start.5 = (s32[128,8]{0,1:T(8,128)S(1)}, s32[128,8]{0,1:T(8,128)}, u32[]{:S(2)}) copy-start(s32[128,8]{0,1:T(8,128)} %param.8) | copy-start | bytes 12292
  3.7 0.7 %copy-start.6 = (f32[128,8]{0,1:T(8,128)S(1)}, f32[128,8]{0,1:T(8,128)}, u32[]{:S(2)}) copy-start(f32[128,8]{0,1:T(8,128)} %param.9) | copy-start | bytes 12292
  4.4 29.1 %copy-start = (bf16[1,256,3584]{2,1,0:T(8,128)(2,1)S(1)}, bf16[1,256,3584]{2,1,0:T(8,128)(2,1)}, u32[]{:S(2)}) copy-start(bf16[1,256,3584]{2,1,0:T(8,128)(2,1)} %param.11) | copy-start | bytes 5505028
  33.5 1.5 %copy-start.1 = (bf16[1,256,3584]{2,1,0:T(8,128)(2,1)S(1)}, bf16[1,256,3584]{2,1,0:T(8,128)(2,1)}, u32[]{:S(2)}) copy-start(bf16[1,256,3584]{2,1,0:T(8,128)(2,1)} %param.12) | copy-start | bytes 5505028
  35.0 1.5 %copy-start.2 = (bf16[1,256,3584]{2,1,0:T(8,128)(2,1)S(1)}, bf16[1,256,3584]{2,1,0:T(8,128)(2,1)}, u32[]{:S(2)}) copy-start(bf16[1,256,3584]{2,1,0:T(8,128)(2,1)} %param.13) | copy-start | bytes 5505028

commit v2 on v1

v2 whole, which is shorter than its diff:
```python
import functools

import jax
import jax.numpy as jnp
from jax import lax
from jax.experimental import pallas as pl
from jax.experimental.pallas import tpu as pltpu
from jax.sharding import PartitionSpec as P

CAP = 2
ROWS = 2 * CAP
MIB = 1024 * 1024

VMEM = pl.BlockSpec(memory_space=pltpu.VMEM)
HBM = pl.BlockSpec(memory_space=pltpu.HBM)


def in_hbm(*arrays):
    return [pltpu.with_memory_space_constraint(array, pltpu.HBM) for array in arrays]


def pick_kernel(ids_hbm, probs_hbm, tokens_hbm, grad_hbm, own_ref, other_ref, ids_buf, probs_buf, buf, sems):
    copy_ids = pltpu.make_async_copy(ids_hbm, ids_buf, sems.at[0])
    copy_probs = pltpu.make_async_copy(probs_hbm, probs_buf, sems.at[1])
    copy_ids.start()
    copy_probs.start()
    pieces = (sems.shape[0] - 2) // 2
    top, count = ids_buf.shape
    width = buf.shape[1] // pieces
    copies = []
    for part in range(pieces):
        cols = pl.ds(part * width, width)
        for number, source in enumerate((tokens_hbm, grad_hbm)):
            copy = pltpu.make_async_copy(
                source.at[:, cols], buf.at[pl.ds(number * count, count), cols], sems.at[2 + 2 * part + number]
            )
            copy.start()
            copies.append(copy)
    half = own_ref.shape[0]
    total = 2 * half
    row = lax.broadcasted_iota(jnp.int32, (total, 1), 0)
    block = row // ROWS
    places = total // ROWS // 2
    relative = 2 * (block % places) + block // places
    expert = lax.axis_index("expert") ^ relative
    slot = (row % CAP).astype(jnp.float32)
    is_x = row % ROWS < CAP
    earlier = (
        lax.broadcasted_iota(jnp.int32, (count, count), 0)
        < lax.broadcasted_iota(jnp.int32, (count, count), 1)
    ).astype(jnp.bfloat16)
    copy_ids.wait()
    copy_probs.wait()
    named = jnp.zeros((total, count), jnp.float32)
    prob = jnp.zeros((total, count), jnp.float32)
    for k in range(top):
        hit = ids_buf[k : k + 1, :] == expert
        named = jnp.where(hit, 1.0, named)
        prob = jnp.where(hit, probs_buf[k : k + 1, :], prob)
    rank = jnp.dot(named.astype(jnp.bfloat16), earlier, preferred_element_type=jnp.float32)
    pick = jnp.where((named > 0.5) & (rank == slot), 1.0, 0.0)
    scale = jnp.where(is_x, 1.0, jnp.sum(pick * prob, axis=1, keepdims=True))
    picker = jnp.concatenate([jnp.where(is_x, pick, 0.0), jnp.where(is_x, 0.0, pick)], axis=1).astype(jnp.bfloat16)
    for part in range(pieces):
        cols = pl.ds(part * width, width)
        copies[2 * part].wait()
        copies[2 * part + 1].wait()
        rows = jnp.dot(picker, buf[:, cols], preferred_element_type=jnp.float32) * scale
        rows = rows.astype(jnp.bfloat16)
        own_ref[:, cols] = rows[:half]
        other_ref[:, cols] = rows[half:]


def pick_rows(experts, ids, probs, tokens, out_grad):
    top = ids.shape[0]
    count, channels = tokens.shape
    pieces = 4
    shape = pltpu.VMEM((experts * ROWS // 2, channels), jnp.bfloat16)
    return pl.pallas_call(
        pick_kernel,
        out_shape=(shape, shape),
        in_specs=[HBM] * 4,
        out_specs=(VMEM, VMEM),
        scratch_shapes=[
            pltpu.VMEM((top, count), jnp.int32),
            pltpu.VMEM((top, count), jnp.float32),
            pltpu.VMEM((2 * count, channels), jnp.bfloat16),
            pltpu.SemaphoreType.DMA((2 + 2 * pieces,)),
        ],
        compiler_params=pltpu.CompilerParams(vmem_limit_bytes=16 * MIB),
    )(*in_hbm(ids, probs, tokens, out_grad))


def load_kernel(*refs):
    gate_hbm, up_hbm, down_hbm, gate_ref, up_ref, down_ref, sems = refs[-7:]
    copies = []
    for number, (source, target) in enumerate(((gate_hbm, gate_ref), (up_hbm, up_ref), (down_hbm, down_ref))):
        half = source.shape[0] // 2
        for part in range(2):
            rows = pl.ds(part * half, half)
            copy = pltpu.make_async_copy(source.at[rows], target.at[rows], sems.at[number, part])
            copy.start()
            copies.append(copy)
    for copy in copies:
        copy.wait()


def load_weights(after, w_gate, w_up, w_down):
    shape = pltpu.VMEM(w_gate.shape, w_gate.dtype)
    size = w_gate.size * 2
    return pl.pallas_call(
        load_kernel,
        out_shape=(shape, shape, shape),
        in_specs=[pl.BlockSpec(memory_space=pl.ANY)] * len(after) + [HBM] * 3,
        out_specs=(VMEM, VMEM, VMEM),
        scratch_shapes=[pltpu.SemaphoreType.DMA((3, 2))],
        compiler_params=pltpu.CompilerParams(vmem_limit_bytes=8 * MIB),
        cost_estimate=pl.CostEstimate(flops=0, bytes_accessed=6 * size, transcendentals=0),
    )(*after, *in_hbm(w_gate, w_up, w_down))


def join_kernel(first_ref, second_ref, near_ref, out_ref):
    half = first_ref.shape[0]
    out_ref[:half] = first_ref[...]
    out_ref[half:] = second_ref[...]


def join(first, second, near):
    return pl.pallas_call(
        join_kernel,
        out_shape=pltpu.VMEM((2 * first.shape[0], first.shape[1]), first.dtype),
        in_specs=[VMEM, VMEM, pl.BlockSpec(memory_space=pl.ANY)],
        out_specs=VMEM,
        compiler_params=pltpu.CompilerParams(vmem_limit_bytes=4 * MIB),
    )(first, second, near)


def grads_kernel(pieces_in, *refs):
    parts = refs[:pieces_in]
    gate_ref, up_ref, down_ref, out_gate, out_up, out_down, rows_ref, buf, sems = refs[pieces_in:]
    start = 0
    for part in parts:
        rows_ref[pl.ds(start, part.shape[0])] = part[...]
        start += part.shape[0]
    rows = rows_ref[...]
    count, channels = rows.shape
    contract = (((1,), (1,)), ((), ()))
    gate_pre = lax.dot_general(rows, gate_ref[...], contract, preferred_element_type=jnp.float32)
    up_pre = lax.dot_general(rows, up_ref[...], contract, preferred_element_type=jnp.float32)
    is_x = lax.broadcasted_iota(jnp.int32, (count, 1), 0) % ROWS < CAP
    sig_gate = jax.nn.sigmoid(gate_pre)
    act_gate = gate_pre * sig_gate
    hidden = pltpu.roll(jnp.where(is_x, act_gate * up_pre, 0.0), CAP, 0)
    pieces = sems.shape[1]
    width = channels // pieces
    copies = []

    def outer(number, factor, out):
        turned = factor.T.astype(jnp.bfloat16)
        for part in range(pieces):
            cols = pl.ds(part * width, width)
            term = jnp.dot(turned, rows_ref[:, cols], preferred_element_type=jnp.float32)
            buf[number, :, cols] = term.astype(jnp.bfloat16)
            copy = pltpu.make_async_copy(buf.at[number, :, cols], out.at[:, cols], sems.at[number, part])
            copy.start()
            copies.append(copy)

    outer(0, hidden, out_down)
    back_grad = lax.dot_general(rows, down_ref[...], contract, preferred_element_type=jnp.float32)
    back_grad = pltpu.roll(back_grad, count - CAP, 0)
    outer(1, jnp.where(is_x, back_grad * act_gate, 0.0), out_up)
    d_gate = jnp.where(is_x, back_grad * up_pre * sig_gate * (1.0 + gate_pre * (1.0 - sig_gate)), 0.0)
    outer(2, d_gate, out_gate)
    for copy in copies:
        copy.wait()


def weight_grads(parts, w_gate, w_up, w_down):
    units, channels = w_gate.shape
    count = sum(part.shape[0] for part in parts)
    pieces = 4
    shape = jax.ShapeDtypeStruct((units, channels), jnp.bfloat16)
    return pl.pallas_call(
        functools.partial(grads_kernel, len(parts)),
        out_shape=(shape, shape, shape),
        in_specs=[VMEM] * (len(parts) + 3),
        out_specs=(HBM, HBM, HBM),
        scratch_shapes=[
            pltpu.VMEM((count, channels), jnp.bfloat16),
            pltpu.VMEM((3, units, channels), jnp.bfloat16),
            pltpu.SemaphoreType.DMA((3, pieces)),
        ],
        compiler_params=pltpu.CompilerParams(vmem_limit_bytes=24 * MIB),
    )(*parts, w_gate, w_up, w_down)


def swap(rows, axis, bits):
    count = lax.axis_size(axis)
    return lax.ppermute(rows, axis, [(place, place ^ bits) for place in range(count)])


def spread(rows):
    count = lax.axis_size("dp")
    if count > 4:
        return [lax.all_gather(rows, "dp", axis=0, tiled=True)]
    return [rows] + [swap(rows, "dp", bits) for bits in range(1, count)]


def local(tokens, expert_ids, gate_probs, out_grad, w_gate, w_up, w_down):
    experts = w_gate.shape[0] * lax.axis_size("expert")
    places = experts // 2
    own, other = pick_rows(experts, expert_ids.T, gate_probs.T, tokens, out_grad)
    other = swap(other, "expert", 1)
    blocks = []
    for place in range(places):
        cut = slice(place * ROWS, (place + 1) * ROWS)
        blocks.append(jnp.concatenate([own[cut], other[cut]]))
    arrived = [blocks[0]] + [swap(blocks[place], "expert", 2 * place) for place in range(1, places)]
    arrived[2:] = arrived[:1:-1]
    near = jnp.concatenate(arrived[: places // 2])
    middle = places // 4
    far = [jnp.concatenate(arrived[places // 2 :][:middle]), jnp.concatenate(arrived[places // 2 :][middle:])]
    far = join(far[0], far[1], near)
    parts = spread(near)
    gate, up, down = load_weights(parts + [far], w_gate[0], w_up[0], w_down[0])
    parts = parts + spread(far)
    grads = weight_grads(parts, gate, up, down)
    return tuple(grad[None] for grad in grads)


def solution(mesh):
    in_specs = (
        P(("expert", "dp"), None),
        P(("expert", "dp"), None),
        P(("expert", "dp"), None),
        P(("expert", "dp"), None),
        P("expert", "dp", None),
        P("expert", "dp", None),
        P("expert", "dp", None),
    )
    out_specs = (P("expert", "dp", None), P("expert", "dp", None), P("expert", "dp", None))
    return jax.shard_map(local, mesh=mesh, in_specs=in_specs, out_specs=out_specs, check_vma=False)
```

time: 41.4 us -> 31.1 us (0.75)
  blocking collectives: 27.2 us -> 0 us
  starting transfers between devices: 0 us -> 16.2 us
  local copies, waits for them, and re-layouts: 6.78 us -> 0.08 us
  Pallas kernels: 6.41 us -> 10.2 us
  waiting for transfers between devices: 0 us -> 3.63 us
    ppermute x0 -> x10, starting transfers between devices: none -> 16.2 us  [swap(): lax.ppermute(rows, axis, [(place, place ^ bits) for place in range(count)])]
    all_to_all x1 -> x0, blocking collectives: 15.2 us -> none  [local(): lax.all_to_all(sent, 'expert', split_axis=0, concat_axis=0, tiled=True)]
    all_gather x1 -> x0, blocking collectives: 12 us -> none  [local(): rows = lax.all_gather(recv.reshape(-1, channels), 'dp', axis=0, tiled=True)]
    unnamed x14 -> x0, local copies, waits for them, and re-layouts: 6.72 us -> none
    pallas_call x2 -> x4, Pallas kernels: 6.41 us -> 10.2 us  [the longest x1 5.59 us: weight_grads(): pl.pallas_call(functools.partial(grads_kernel, len(parts)), out_shape=(sh...]
    ppermute x0 -> x10, waiting for transfers between devices: none -> 3.63 us  [swap(): lax.ppermute(rows, axis, [(place, place ^ bits) for place in range(count)])]
  transfers between devices with their start and end apart: 0 -> 10, of which waited for: 0 -> 5; matrix products, arithmetic and copies ran while one was open for 0% -> 1% of each run, Pallas kernels for 0% -> 8%
where the time goes in v2:
time: 31.1 us; the launch traced here: 30.9 us
  starting transfers between devices  16.2 us (52%)
  Pallas kernels  10.2 us (33%)
  waiting for transfers between devices  3.63 us (12%)
  between operations  0.68 us (2%)
    ppermute x10, starting transfers between devices, swap(): lax.ppermute(rows, axis, [(place, place ^ bits) for place in range(count)])  16.2 us
    pallas_call x1, Pallas kernels, weight_grads(): pl.pallas_call(functools.partial(grads_kernel, len(parts)), out_shape=(sh...  5.59 us
    ppermute x10, waiting for transfers between devices, swap(): lax.ppermute(rows, axis, [(place, place ^ bits) for place in range(count)])  3.63 us
    pallas_call x1, Pallas kernels, load_weights(): pl.pallas_call(load_kernel, out_shape=(shape, shape, shape), in_specs=[pl...  2.61 us
    pallas_call x1, Pallas kernels, pick_rows(): pl.pallas_call(pick_kernel, out_shape=(shape, shape), in_specs=[HBM] * 4,...  2 us
  transfers between devices with their start and end apart: 10, of which 5 were waited for; matrix products, arithmetic and copies ran while one was open for 1% of the time, Pallas kernels for 8%

profile of v2, /device:TPU:0, one launch (start us, length us, event | category | flops | bytes accessed | tf_op | source)
XLA Modules:
  0.0 30.9 jit_solution(14698200873342481772)
XLA Ops:
  0.6 2.0 %shard_map.94 = (bf16[16,3584]{1,0:T(8,128)(2,1)S(1)}, bf16[16,3584]{1,0:T(8,128)(2,1)S(1)}) custom-call(s32[8,128]{1,0:T(8,128)} %bitcast.11, f32[8,128]{1,0:T(8,128)} %bitcast.12, bf16[128,3584]{1,0:T(8,128)(2,1)} %tokens_hbm.1, bf16[128,3584]{1,0:T(8,128)(2,1)} %grad_hbm.1), custom_call_target="tpu_custom_call" | custom-call | tf_op jit(solution)/shard_map/pallas_call | solution.py:79
  2.6 0.5 %collective-permute-start = (bf16[16,3584]{1,0:T(8,128)(2,1)S(1)}, bf16[16,3584]{1,0:T(8,128)(2,1)S(1)}, u32[]{:S(2)}, u32[]{:S(2)}) collective-permute-start(bf16[16,3584]{1,0:T(8,128)(2,1)S(1)} %get-tuple-element.12), channel_id=1, source_target_pairs={{0,4},{4,0},{8,12},{12,8},{16,20},{20,16},{24,28},{28,24},{1,5},{5... | collective-permute-start | bytes 344072 | tf_op jit(solution)/shard_map/ppermute | solution.py:199
  3.2 0.9 %collective-permute-done = bf16[16,3584]{1,0:T(8,128)(2,1)S(1)} collective-permute-done((bf16[16,3584]{1,0:T(8,128)(2,1)S(1)}, bf16[16,3584]{1,0:T(8,128)(2,1)S(1)}, u32[]{:S(2)}, u32[]{:S(2)}) %collective-permute-start) | collective-permute-done | bytes 114720 | tf_op jit(solution)/shard_map/ppermute | solution.py:199
  4.2 3.0 %collective-permute-start.1 = (bf16[8,3584]{1,0:T(8,128)(2,1)S(1)}, bf16[8,3584]{1,0:T(8,128)(2,1)S(1)}, u32[]{:S(2)}, u32[]{:S(2)}) collective-permute-start(bf16[8,3584]{1,0:T(8,128)(2,1)S(1)} %pad_maximum_fusion.1), channel_id=1, source_target_pairs={{0,8},{4,12},{8,0},{12,4},{16,24},{20,28},{24,16},{28,20},{1,9},{5... | collective-permute-start | bytes 172040 | tf_op jit(solution)/shard_map/ppermute | solution.py:199
  7.2 2.5 %collective-permute-start.5 = (bf16[8,3584]{1,0:T(8,128)(2,1)S(1)}, bf16[8,3584]{1,0:T(8,128)(2,1)S(1)}, u32[]{:S(2)}, u32[]{:S(2)}) collective-permute-start(bf16[8,3584]{1,0:T(8,128)(2,1)S(1)} %pad_maximum_fusion.2), channel_id=1, source_target_pairs={{0,24},{4,28},{8,16},{12,20},{16,8},{20,12},{24,0},{28,4},{1,25},{... | collective-permute-start | bytes 172040 | tf_op jit(solution)/shard_map/ppermute | solution.py:199
  9.8 0.0 collective-permute-done.1
  9.8 0.1 pad_maximum_fusion.near_ref.refs_0_
  9.8 2.5 %collective-permute-start.4 = (bf16[16,3584]{1,0:T(8,128)(2,1)S(1)}, bf16[16,3584]{1,0:T(8,128)(2,1)S(1)}, u32[]{:S(2)}, u32[]{:S(2)}) collective-permute-start(bf16[16,3584]{1,0:T(8,128)(2,1)S(1)} %pad_maximum_fusion.near_ref.refs_0_), channel_id=1, source_target_pairs={{0,3},{1,2},{2,1},{3,0},{4,7},{5,6},{6,5},{7,4},{8,11},{9,10},{10,... | collective-permute-start | bytes 344072 | tf_op jit(solution)/shard_map/ppermute | solution.py:199
  12.4 3.0 %collective-permute-start.6 = (bf16[8,3584]{1,0:T(8,128)(2,1)S(1)}, bf16[8,3584]{1,0:T(8,128)(2,1)S(1)}, u32[]{:S(2)}, u32[]{:S(2)}) collective-permute-start(bf16[8,3584]{1,0:T(8,128)(2,1)S(1)} %pad_maximum_fusion.3), channel_id=1, source_target_pairs={{0,16},{4,20},{8,24},{12,28},{16,0},{20,4},{24,8},{28,12},{1,17},{... | collective-permute-start | bytes 172040 | tf_op jit(solution)/shard_map/ppermute | solution.py:199
  15.4 0.5 %collective-permute-start.3 = (bf16[16,3584]{1,0:T(8,128)(2,1)S(1)}, bf16[16,3584]{1,0:T(8,128)(2,1)S(1)}, u32[]{:S(2)}, u32[]{:S(2)}) collective-permute-start(bf16[16,3584]{1,0:T(8,128)(2,1)S(1)} %pad_maximum_fusion.near_ref.refs_0_), channel_id=1, source_target_pairs={{0,2},{1,3},{2,0},{3,1},{4,6},{5,7},{6,4},{7,5},{8,10},{9,11},{10,... | collective-permute-start | bytes 344072 | tf_op jit(solution)/shard_map/ppermute | solution.py:199
  15.9 0.5 %collective-permute-start.2 = (bf16[16,3584]{1,0:T(8,128)(2,1)S(1)}, bf16[16,3584]{1,0:T(8,128)(2,1)S(1)}, u32[]{:S(2)}, u32[]{:S(2)}) collective-permute-start(bf16[16,3584]{1,0:T(8,128)(2,1)S(1)} %pad_maximum_fusion.near_ref.refs_0_), channel_id=1, source_target_pairs={{0,1},{1,0},{2,3},{3,2},{4,5},{5,4},{6,7},{7,6},{8,9},{9,8},{10,11... | collective-permute-start | bytes 344072 | tf_op jit(solution)/shard_map/ppermute | solution.py:199
  16.5 0.0 collective-permute-done.5.first_ref
  16.5 1.1 %collective-permute-done.6.second_ref = bf16[8,3584]{1,0:T(8,128)(2,1)S(1)} collective-permute-done((bf16[8,3584]{1,0:T(8,128)(2,1)S(1)}, bf16[8,3584]{1,0:T(8,128)(2,1)S(1)}, u32[]{:S(2)}, u32[]{:S(2)}) %collective-permute-start.6) | collective-permute-done | bytes 57376 | tf_op jit(solution)/shard_map/ppermute | solution.py:199
  17.6 1.4 %collective-permute-start.9 = (bf16[16,3584]{1,0:T(8,128)(2,1)S(1)}, bf16[16,3584]{1,0:T(8,128)(2,1)S(1)}, u32[]{:S(2)}, u32[]{:S(2)}) collective-permute-start(bf16[16,3584]{1,0:T(8,128)(2,1)S(1)} %shard_map.95.refs_4_), channel_id=1, source_target_pairs={{0,3},{1,2},{2,1},{3,0},{4,7},{5,6},{6,5},{7,4},{8,11},{9,10},{10,... | collective-permute-start | bytes 344072 | tf_op jit(solution)/shard_map/ppermute | solution.py:199
  19.0 0.7 %collective-permute-start.8 = (bf16[16,3584]{1,0:T(8,128)(2,1)S(1)}, bf16[16,3584]{1,0:T(8,128)(2,1)S(1)}, u32[]{:S(2)}, u32[]{:S(2)}) collective-permute-start(bf16[16,3584]{1,0:T(8,128)(2,1)S(1)} %shard_map.95.refs_4_), channel_id=1, source_target_pairs={{0,2},{1,3},{2,0},{3,1},{4,6},{5,7},{6,4},{7,5},{8,10},{9,11},{10,... | collective-permute-start | bytes 344072 | tf_op jit(solution)/shard_map/ppermute | solution.py:199
  19.6 0.0 collective-permute-done.4.refs_3_
  19.7 1.5 %collective-permute-start.7 = (bf16[16,3584]{1,0:T(8,128)(2,1)S(1)}, bf16[16,3584]{1,0:T(8,128)(2,1)S(1)}, u32[]{:S(2)}, u32[]{:S(2)}) collective-permute-start(bf16[16,3584]{1,0:T(8,128)(2,1)S(1)} %shard_map.95.refs_4_), channel_id=1, source_target_pairs={{0,1},{1,0},{2,3},{3,2},{4,5},{5,4},{6,7},{7,6},{8,9},{9,8},{10,11... | collective-permute-start | bytes 344072 | tf_op jit(solution)/shard_map/ppermute | solution.py:199
  21.1 1.1 %collective-permute-done.3.refs_2_ = bf16[16,3584]{1,0:T(8,128)(2,1)S(1)} collective-permute-done((bf16[16,3584]{1,0:T(8,128)(2,1)S(1)}, bf16[16,3584]{1,0:T(8,128)(2,1)S(1)}, u32[]{:S(2)}, u32[]{:S(2)}) %collective-permute-start.3) | collective-permute-done | bytes 114720 | tf_op jit(solution)/shard_map/ppermute | solution.py:199
  22.2 0.0 collective-permute-done.2.refs_1_
  22.2 2.6 %shard_map.96 = (bf16[256,3584]{1,0:T(8,128)(2,1)S(1)}, bf16[256,3584]{1,0:T(8,128)(2,1)S(1)}, bf16[256,3584]{1,0:T(8,128)(2,1)S(1)}) custom-call(bf16[16,3584]{1,0:T(8,128)(2,1)S(1)} %pad_maximum_fusion.near_ref.refs_0_, bf16[16,3584]{1,0:T(8,128)(2,1)S(1)} %collective-permute-done.2.refs_1_, bf16[16,3584]{1,0:T(8,128)(2,1)S(1)} %collective-permute-done.3.refs_2_, ...), custom_call_target="tpu_custom_call" | custom-call | bytes 11010048 | tf_op jit(solution)/shard_map/pallas_call | solution.py:111
  24.9 0.0 collective-permute-done.9.refs_7_
  24.9 0.2 collective-permute-done.8.refs_6_
  25.1 0.2 collective-permute-done.7.refs_5_
  25.4 5.6 %shard_map.97 = (bf16[256,3584]{1,0:T(8,128)(2,1)}, bf16[256,3584]{1,0:T(8,128)(2,1)}, bf16[256,3584]{1,0:T(8,128)(2,1)}) custom-call(bf16[16,3584]{1,0:T(8,128)(2,1)S(1)} %pad_maximum_fusion.near_ref.refs_0_, bf16[16,3584]{1,0:T(8,128)(2,1)S(1)} %collective-permute-done.2.refs_1_, bf16[16,3584]{1,0:T(8,128)(2,1)S(1)} %collective-permute-done.3.refs_2_, ...), custom_call_target="tpu_custom_call" | custom-call | tf_op jit(solution)/shard_map/pallas_call | solution.py:183
  (6 shorter events, 0.2 us)
Async XLA Ops:
  2.6 1.5 %collective-permute-start = (bf16[16,3584]{1,0:T(8,128)(2,1)S(1)}, bf16[16,3584]{1,0:T(8,128)(2,1)S(1)}, u32[]{:S(2)}, u32[]{:S(2)}) collective-permute-start(bf16[16,3584]{1,0:T(8,128)(2,1)S(1)} %get-tuple-element.12), channel_id=1, source_target_pairs={{0,4},{4,0},{8,12},{12,8},{16,20},{20,16},{24,28},{28,24},{1,5},{5... | collective-permute-start | bytes 344072 | tf_op jit(solution)/shard_map/ppermute | solution.py:199
  4.2 5.6 %collective-permute-start.1 = (bf16[8,3584]{1,0:T(8,128)(2,1)S(1)}, bf16[8,3584]{1,0:T(8,128)(2,1)S(1)}, u32[]{:S(2)}, u32[]{:S(2)}) collective-permute-start(bf16[8,3584]{1,0:T(8,128)(2,1)S(1)} %pad_maximum_fusion.1), channel_id=1, source_target_pairs={{0,8},{4,12},{8,0},{12,4},{16,24},{20,28},{24,16},{28,20},{1,9},{5... | collective-permute-start | bytes 172040 | tf_op jit(solution)/shard_map/ppermute | solution.py:199
  7.2 9.2 %collective-permute-start.5 = (bf16[8,3584]{1,0:T(8,128)(2,1)S(1)}, bf16[8,3584]{1,0:T(8,128)(2,1)S(1)}, u32[]{:S(2)}, u32[]{:S(2)}) collective-permute-start(bf16[8,3584]{1,0:T(8,128)(2,1)S(1)} %pad_maximum_fusion.2), channel_id=1, source_target_pairs={{0,24},{4,28},{8,16},{12,20},{16,8},{20,12},{24,0},{28,4},{1,25},{... | collective-permute-start | bytes 172040 | tf_op jit(solution)/shard_map/ppermute | solution.py:199
  9.8 9.8 %collective-permute-start.4 = (bf16[16,3584]{1,0:T(8,128)(2,1)S(1)}, bf16[16,3584]{1,0:T(8,128)(2,1)S(1)}, u32[]{:S(2)}, u32[]{:S(2)}) collective-permute-start(bf16[16,3584]{1,0:T(8,128)(2,1)S(1)} %pad_maximum_fusion.near_ref.refs_0_), channel_id=1, source_target_pairs={{0,3},{1,2},{2,1},{3,0},{4,7},{5,6},{6,5},{7,4},{8,11},{9,10},{10,... | collective-permute-start | bytes 344072 | tf_op jit(solution)/shard_map/ppermute | solution.py:199
  12.4 5.2 %collective-permute-start.6 = (bf16[8,3584]{1,0:T(8,128)(2,1)S(1)}, bf16[8,3584]{1,0:T(8,128)(2,1)S(1)}, u32[]{:S(2)}, u32[]{:S(2)}) collective-permute-start(bf16[8,3584]{1,0:T(8,128)(2,1)S(1)} %pad_maximum_fusion.3), channel_id=1, source_target_pairs={{0,16},{4,20},{8,24},{12,28},{16,0},{20,4},{24,8},{28,12},{1,17},{... | collective-permute-start | bytes 172040 | tf_op jit(solution)/shard_map/ppermute | solution.py:199
  15.4 6.8 %collective-permute-start.3 = (bf16[16,3584]{1,0:T(8,128)(2,1)S(1)}, bf16[16,3584]{1,0:T(8,128)(2,1)S(1)}, u32[]{:S(2)}, u32[]{:S(2)}) collective-permute-start(bf16[16,3584]{1,0:T(8,128)(2,1)S(1)} %pad_maximum_fusion.near_ref.refs_0_), channel_id=1, source_target_pairs={{0,2},{1,3},{2,0},{3,1},{4,6},{5,7},{6,4},{7,5},{8,10},{9,11},{10,... | collective-permute-start | bytes 344072 | tf_op jit(solution)/shard_map/ppermute | solution.py:199
  15.9 6.3 %collective-permute-start.2 = (bf16[16,3584]{1,0:T(8,128)(2,1)S(1)}, bf16[16,3584]{1,0:T(8,128)(2,1)S(1)}, u32[]{:S(2)}, u32[]{:S(2)}) collective-permute-start(bf16[16,3584]{1,0:T(8,128)(2,1)S(1)} %pad_maximum_fusion.near_ref.refs_0_), channel_id=1, source_target_pairs={{0,1},{1,0},{2,3},{3,2},{4,5},{5,4},{6,7},{7,6},{8,9},{9,8},{10,11... | collective-permute-start | bytes 344072 | tf_op jit(solution)/shard_map/ppermute | solution.py:199
  17.6 7.3 %collective-permute-start.9 = (bf16[16,3584]{1,0:T(8,128)(2,1)S(1)}, bf16[16,3584]{1,0:T(8,128)(2,1)S(1)}, u32[]{:S(2)}, u32[]{:S(2)}) collective-permute-start(bf16[16,3584]{1,0:T(8,128)(2,1)S(1)} %shard_map.95.refs_4_), channel_id=1, source_target_pairs={{0,3},{1,2},{2,1},{3,0},{4,7},{5,6},{6,5},{7,4},{8,11},{9,10},{10,... | collective-permute-start | bytes 344072 | tf_op jit(solution)/shard_map/ppermute | solution.py:199
  19.0 6.1 %collective-permute-start.8 = (bf16[16,3584]{1,0:T(8,128)(2,1)S(1)}, bf16[16,3584]{1,0:T(8,128)(2,1)S(1)}, u32[]{:S(2)}, u32[]{:S(2)}) collective-permute-start(bf16[16,3584]{1,0:T(8,128)(2,1)S(1)} %shard_map.95.refs_4_), channel_id=1, source_target_pairs={{0,2},{1,3},{2,0},{3,1},{4,6},{5,7},{6,4},{7,5},{8,10},{9,11},{10,... | collective-permute-start | bytes 344072 | tf_op jit(solution)/shard_map/ppermute | solution.py:199
  19.7 5.7 %collective-permute-start.7 = (bf16[16,3584]{1,0:T(8,128)(2,1)S(1)}, bf16[16,3584]{1,0:T(8,128)(2,1)S(1)}, u32[]{:S(2)}, u32[]{:S(2)}) collective-permute-start(bf16[16,3584]{1,0:T(8,128)(2,1)S(1)} %shard_map.95.refs_4_), channel_id=1, source_target_pairs={{0,1},{1,0},{2,3},{3,2},{4,5},{5,4},{6,7},{7,6},{8,9},{9,8},{10,11... | collective-permute-start | bytes 344072 | tf_op jit(solution)/shard_map/ppermute | solution.py:199

commit v3 on v2

--- a/solution.py
+++ b/solution.py
@@ -132,6 +132,7 @@
         in_specs=[VMEM, VMEM, pl.BlockSpec(memory_space=pl.ANY)],
         out_specs=VMEM,
         compiler_params=pltpu.CompilerParams(vmem_limit_bytes=4 * MIB),
+        cost_estimate=pl.CostEstimate(flops=10**9, bytes_accessed=0, transcendentals=0),
     )(first, second, near)
 
 
@@ -145,29 +146,28 @@
     rows = rows_ref[...]
     count, channels = rows.shape
     contract = (((1,), (1,)), ((), ()))
-    gate_pre = lax.dot_general(rows, gate_ref[...], contract, preferred_element_type=jnp.float32)
-    up_pre = lax.dot_general(rows, up_ref[...], contract, preferred_element_type=jnp.float32)
-    is_x = lax.broadcasted_iota(jnp.int32, (count, 1), 0) % ROWS < CAP
+    gate_pre = lax.dot_general(gate_ref[...], rows, contract, preferred_element_type=jnp.float32)
+    up_pre = lax.dot_general(up_ref[...], rows, contract, preferred_element_type=jnp.float32)
+    back_grad = lax.dot_general(down_ref[...], rows, contract, preferred_element_type=jnp.float32)
+    back_grad = pltpu.roll(back_grad, count - CAP, 1)
+    is_x = lax.broadcasted_iota(jnp.int32, (1, count), 1) % ROWS < CAP
     sig_gate = jax.nn.sigmoid(gate_pre)
     act_gate = gate_pre * sig_gate
-    hidden = pltpu.roll(jnp.where(is_x, act_gate * up_pre, 0.0), CAP, 0)
     pieces = sems.shape[1]
     width = channels // pieces
     copies = []
 
     def outer(number, factor, out):
-        turned = factor.T.astype(jnp.bfloat16)
+        factor = factor.astype(jnp.bfloat16)
         for part in range(pieces):
             cols = pl.ds(part * width, width)
-            term = jnp.dot(turned, rows_ref[:, cols], preferred_element_type=jnp.float32)
+            term = jnp.dot(factor, rows_ref[:, cols], preferred_element_type=jnp.float32)
             buf[number, :, cols] = term.astype(jnp.bfloat16)
             copy = pltpu.make_async_copy(buf.at[number, :, cols], out.at[:, cols], sems.at[number, part])
             copy.start()
             copies.append(copy)
 
-    outer(0, hidden, out_down)
-    back_grad = lax.dot_general(rows, down_ref[...], contract, preferred_element_type=jnp.float32)
-    back_grad = pltpu.roll(back_grad, count - CAP, 0)
+    outer(0, pltpu.roll(jnp.where(is_x, act_gate * up_pre, 0.0), CAP, 1), out_down)
     outer(1, jnp.where(is_x, back_grad * act_gate, 0.0), out_up)
     d_gate = jnp.where(is_x, back_grad * up_pre * sig_gate * (1.0 + gate_pre * (1.0 - sig_gate)), 0.0)
     outer(2, d_gate, out_gate)
@@ -216,7 +216,6 @@
         cut = slice(place * ROWS, (place + 1) * ROWS)
         blocks.append(jnp.concatenate([own[cut], other[cut]]))
     arrived = [blocks[0]] + [swap(blocks[place], "expert", 2 * place) for place in range(1, places)]
-    arrived[2:] = arrived[:1:-1]
     near = jnp.concatenate(arrived[: places // 2])
     middle = places // 4
     far = [jnp.concatenate(arrived[places // 2 :][:middle]), jnp.concatenate(arrived[places // 2 :][middle:])]

time: 31.1 us -> 28.2 us (0.907)
  starting transfers between devices: 16.2 us -> 13.3 us
  Pallas kernels: 10.2 us -> 8.88 us
  waiting for transfers between devices: 3.63 us -> 4.9 us
    ppermute x10, starting transfers between devices: 16.2 us -> 13.3 us  [swap(): lax.ppermute(rows, axis, [(place, place ^ bits) for place in range(count)])]
    pallas_call x1, Pallas kernels: 5.59 us -> 4.26 us  [weight_grads(): pl.pallas_call(functools.partial(grads_kernel, len(parts)), out_shape=(sh...]
    ppermute x10, waiting for transfers between devices: 3.63 us -> 4.9 us  [swap(): lax.ppermute(rows, axis, [(place, place ^ bits) for place in range(count)])]
  transfers between devices with their start and end apart: 10 -> 10, of which waited for: 5 -> 5; matrix products, arithmetic and copies ran while one was open for 1% -> 1% of each run, Pallas kernels for 8% -> 9%
where the time goes in v3:
time: 28.2 us; the launch traced here: 28.1 us
  starting transfers between devices  13.3 us (47%)
  Pallas kernels  8.88 us (31%)
  waiting for transfers between devices  4.9 us (17%)
  between operations  0.7 us (2%)
    ppermute x10, starting transfers between devices, swap(): lax.ppermute(rows, axis, [(place, place ^ bits) for place in range(count)])  13.3 us
    ppermute x10, waiting for transfers between devices, swap(): lax.ppermute(rows, axis, [(place, place ^ bits) for place in range(count)])  4.9 us
    pallas_call x1, Pallas kernels, weight_grads(): pl.pallas_call(functools.partial(grads_kernel, len(parts)), out_shape=(sh...  4.26 us
    pallas_call x1, Pallas kernels, load_weights(): pl.pallas_call(load_kernel, out_shape=(shape, shape, shape), in_specs=[pl...  2.61 us
    pallas_call x1, Pallas kernels, pick_rows(): pl.pallas_call(pick_kernel, out_shape=(shape, shape), in_specs=[HBM] * 4,...  2 us
  transfers between devices with their start and end apart: 10, of which 5 were waited for; matrix products, arithmetic and copies ran while one was open for 1% of the time, Pallas kernels for 9%

profile of v3, /device:TPU:0, one launch (start us, length us, event | category | flops | bytes accessed | tf_op | source)
XLA Modules:
  0.0 28.1 jit_solution(2577478494039367312)
XLA Ops:
  0.6 2.0 %shard_map.94 = (bf16[16,3584]{1,0:T(8,128)(2,1)S(1)}, bf16[16,3584]{1,0:T(8,128)(2,1)S(1)}) custom-call(s32[8,128]{1,0:T(8,128)} %bitcast.11, f32[8,128]{1,0:T(8,128)} %bitcast.12, bf16[128,3584]{1,0:T(8,128)(2,1)} %tokens_hbm.1, bf16[128,3584]{1,0:T(8,128)(2,1)} %grad_hbm.1), custom_call_target="tpu_custom_call" | custom-call | tf_op jit(solution)/shard_map/pallas_call | solution.py:79
  2.6 0.5 %collective-permute-start = (bf16[16,3584]{1,0:T(8,128)(2,1)S(1)}, bf16[16,3584]{1,0:T(8,128)(2,1)S(1)}, u32[]{:S(2)}, u32[]{:S(2)}) collective-permute-start(bf16[16,3584]{1,0:T(8,128)(2,1)S(1)} %get-tuple-element.12), channel_id=1, source_target_pairs={{0,4},{4,0},{8,12},{12,8},{16,20},{20,16},{24,28},{28,24},{1,5},{5... | collective-permute-start | bytes 344072 | tf_op jit(solution)/shard_map/ppermute | solution.py:199
  3.2 0.9 %collective-permute-done = bf16[16,3584]{1,0:T(8,128)(2,1)S(1)} collective-permute-done((bf16[16,3584]{1,0:T(8,128)(2,1)S(1)}, bf16[16,3584]{1,0:T(8,128)(2,1)S(1)}, u32[]{:S(2)}, u32[]{:S(2)}) %collective-permute-start) | collective-permute-done | bytes 114720 | tf_op jit(solution)/shard_map/ppermute | solution.py:199
  4.2 3.0 %collective-permute-start.1 = (bf16[8,3584]{1,0:T(8,128)(2,1)S(1)}, bf16[8,3584]{1,0:T(8,128)(2,1)S(1)}, u32[]{:S(2)}, u32[]{:S(2)}) collective-permute-start(bf16[8,3584]{1,0:T(8,128)(2,1)S(1)} %pad_maximum_fusion.1), channel_id=1, source_target_pairs={{0,8},{4,12},{8,0},{12,4},{16,24},{20,28},{24,16},{28,20},{1,9},{5... | collective-permute-start | bytes 172040 | tf_op jit(solution)/shard_map/ppermute | solution.py:199
  7.2 2.7 %collective-permute-start.5 = (bf16[8,3584]{1,0:T(8,128)(2,1)S(1)}, bf16[8,3584]{1,0:T(8,128)(2,1)S(1)}, u32[]{:S(2)}, u32[]{:S(2)}) collective-permute-start(bf16[8,3584]{1,0:T(8,128)(2,1)S(1)} %pad_maximum_fusion.2), channel_id=1, source_target_pairs={{0,16},{4,20},{8,24},{12,28},{16,0},{20,4},{24,8},{28,12},{1,17},{... | collective-permute-start | bytes 172040 | tf_op jit(solution)/shard_map/ppermute | solution.py:199
  9.9 0.1 collective-permute-start.6
  10.0 0.0 collective-permute-done.1
  10.0 0.1 pad_maximum_fusion.near_ref.refs_0_
  10.1 2.7 %collective-permute-start.4 = (bf16[16,3584]{1,0:T(8,128)(2,1)S(1)}, bf16[16,3584]{1,0:T(8,128)(2,1)S(1)}, u32[]{:S(2)}, u32[]{:S(2)}) collective-permute-start(bf16[16,3584]{1,0:T(8,128)(2,1)S(1)} %pad_maximum_fusion.near_ref.refs_0_), channel_id=1, source_target_pairs={{0,3},{1,2},{2,1},{3,0},{4,7},{5,6},{6,5},{7,4},{8,11},{9,10},{10,... | collective-permute-start | bytes 344072 | tf_op jit(solution)/shard_map/ppermute | solution.py:199
  12.8 0.5 %collective-permute-start.3 = (bf16[16,3584]{1,0:T(8,128)(2,1)S(1)}, bf16[16,3584]{1,0:T(8,128)(2,1)S(1)}, u32[]{:S(2)}, u32[]{:S(2)}) collective-permute-start(bf16[16,3584]{1,0:T(8,128)(2,1)S(1)} %pad_maximum_fusion.near_ref.refs_0_), channel_id=1, source_target_pairs={{0,2},{1,3},{2,0},{3,1},{4,6},{5,7},{6,4},{7,5},{8,10},{9,11},{10,... | collective-permute-start | bytes 344072 | tf_op jit(solution)/shard_map/ppermute | solution.py:199
  13.3 0.3 %collective-permute-start.2 = (bf16[16,3584]{1,0:T(8,128)(2,1)S(1)}, bf16[16,3584]{1,0:T(8,128)(2,1)S(1)}, u32[]{:S(2)}, u32[]{:S(2)}) collective-permute-start(bf16[16,3584]{1,0:T(8,128)(2,1)S(1)} %pad_maximum_fusion.near_ref.refs_0_), channel_id=1, source_target_pairs={{0,1},{1,0},{2,3},{3,2},{4,5},{5,4},{6,7},{7,6},{8,9},{9,8},{10,11... | collective-permute-start | bytes 344072 | tf_op jit(solution)/shard_map/ppermute | solution.py:199
  13.6 0.0 collective-permute-done.5.first_ref
  13.6 2.3 %collective-permute-done.6.second_ref = bf16[8,3584]{1,0:T(8,128)(2,1)S(1)} collective-permute-done((bf16[8,3584]{1,0:T(8,128)(2,1)S(1)}, bf16[8,3584]{1,0:T(8,128)(2,1)S(1)}, u32[]{:S(2)}, u32[]{:S(2)}) %collective-permute-start.6) | collective-permute-done | bytes 57376 | tf_op jit(solution)/shard_map/ppermute | solution.py:199
  16.0 2.5 %collective-permute-start.9 = (bf16[16,3584]{1,0:T(8,128)(2,1)S(1)}, bf16[16,3584]{1,0:T(8,128)(2,1)S(1)}, u32[]{:S(2)}, u32[]{:S(2)}) collective-permute-start(bf16[16,3584]{1,0:T(8,128)(2,1)S(1)} %shard_map.95.refs_4_), channel_id=1, source_target_pairs={{0,3},{1,2},{2,1},{3,0},{4,7},{5,6},{6,5},{7,4},{8,11},{9,10},{10,... | collective-permute-start | bytes 344072 | tf_op jit(solution)/shard_map/ppermute | solution.py:199
  18.5 0.5 %collective-permute-start.8 = (bf16[16,3584]{1,0:T(8,128)(2,1)S(1)}, bf16[16,3584]{1,0:T(8,128)(2,1)S(1)}, u32[]{:S(2)}, u32[]{:S(2)}) collective-permute-start(bf16[16,3584]{1,0:T(8,128)(2,1)S(1)} %shard_map.95.refs_4_), channel_id=1, source_target_pairs={{0,2},{1,3},{2,0},{3,1},{4,6},{5,7},{6,4},{7,5},{8,10},{9,11},{10,... | collective-permute-start | bytes 344072 | tf_op jit(solution)/shard_map/ppermute | solution.py:199
  19.0 0.0 collective-permute-done.4.refs_3_
  19.0 0.5 %collective-permute-start.7 = (bf16[16,3584]{1,0:T(8,128)(2,1)S(1)}, bf16[16,3584]{1,0:T(8,128)(2,1)S(1)}, u32[]{:S(2)}, u32[]{:S(2)}) collective-permute-start(bf16[16,3584]{1,0:T(8,128)(2,1)S(1)} %shard_map.95.refs_4_), channel_id=1, source_target_pairs={{0,1},{1,0},{2,3},{3,2},{4,5},{5,4},{6,7},{7,6},{8,9},{9,8},{10,11... | collective-permute-start | bytes 344072 | tf_op jit(solution)/shard_map/ppermute | solution.py:199
  19.5 0.0 collective-permute-done.3.refs_2_
  19.5 0.0 collective-permute-done.2.refs_1_
  19.6 2.6 %shard_map.96 = (bf16[256,3584]{1,0:T(8,128)(2,1)S(1)}, bf16[256,3584]{1,0:T(8,128)(2,1)S(1)}, bf16[256,3584]{1,0:T(8,128)(2,1)S(1)}) custom-call(bf16[16,3584]{1,0:T(8,128)(2,1)S(1)} %pad_maximum_fusion.near_ref.refs_0_, bf16[16,3584]{1,0:T(8,128)(2,1)S(1)} %collective-permute-done.2.refs_1_, bf16[16,3584]{1,0:T(8,128)(2,1)S(1)} %collective-permute-done.3.refs_2_, ...), custom_call_target="tpu_custom_call" | custom-call | bytes 11010048 | tf_op jit(solution)/shard_map/pallas_call | solution.py:111
  22.2 0.8 %collective-permute-done.9.refs_7_ = bf16[16,3584]{1,0:T(8,128)(2,1)S(1)} collective-permute-done((bf16[16,3584]{1,0:T(8,128)(2,1)S(1)}, bf16[16,3584]{1,0:T(8,128)(2,1)S(1)}, u32[]{:S(2)}, u32[]{:S(2)}) %collective-permute-start.9) | collective-permute-done | bytes 114720 | tf_op jit(solution)/shard_map/ppermute | solution.py:199
  22.9 0.8 %collective-permute-done.8.refs_6_ = bf16[16,3584]{1,0:T(8,128)(2,1)S(1)} collective-permute-done((bf16[16,3584]{1,0:T(8,128)(2,1)S(1)}, bf16[16,3584]{1,0:T(8,128)(2,1)S(1)}, u32[]{:S(2)}, u32[]{:S(2)}) %collective-permute-start.8) | collective-permute-done | bytes 114720 | tf_op jit(solution)/shard_map/ppermute | solution.py:199
  23.7 0.1 collective-permute-done.7.refs_5_
  23.8 4.3 %shard_map.97 = (bf16[256,3584]{1,0:T(8,128)(2,1)}, bf16[256,3584]{1,0:T(8,128)(2,1)}, bf16[256,3584]{1,0:T(8,128)(2,1)}) custom-call(bf16[16,3584]{1,0:T(8,128)(2,1)S(1)} %pad_maximum_fusion.near_ref.refs_0_, bf16[16,3584]{1,0:T(8,128)(2,1)S(1)} %collective-permute-done.2.refs_1_, bf16[16,3584]{1,0:T(8,128)(2,1)S(1)} %collective-permute-done.3.refs_2_, ...), custom_call_target="tpu_custom_call" | custom-call | tf_op jit(solution)/shard_map/pallas_call | solution.py:183
  (6 shorter events, 0.2 us)
Async XLA Ops:
  2.6 1.5 %collective-permute-start = (bf16[16,3584]{1,0:T(8,128)(2,1)S(1)}, bf16[16,3584]{1,0:T(8,128)(2,1)S(1)}, u32[]{:S(2)}, u32[]{:S(2)}) collective-permute-start(bf16[16,3584]{1,0:T(8,128)(2,1)S(1)} %get-tuple-element.12), channel_id=1, source_target_pairs={{0,4},{4,0},{8,12},{12,8},{16,20},{20,16},{24,28},{28,24},{1,5},{5... | collective-permute-start | bytes 344072 | tf_op jit(solution)/shard_map/ppermute | solution.py:199
  4.2 5.8 %collective-permute-start.1 = (bf16[8,3584]{1,0:T(8,128)(2,1)S(1)}, bf16[8,3584]{1,0:T(8,128)(2,1)S(1)}, u32[]{:S(2)}, u32[]{:S(2)}) collective-permute-start(bf16[8,3584]{1,0:T(8,128)(2,1)S(1)} %pad_maximum_fusion.1), channel_id=1, source_target_pairs={{0,8},{4,12},{8,0},{12,4},{16,24},{20,28},{24,16},{28,20},{1,9},{5... | collective-permute-start | bytes 172040 | tf_op jit(solution)/shard_map/ppermute | solution.py:199
  7.2 6.4 %collective-permute-start.5 = (bf16[8,3584]{1,0:T(8,128)(2,1)S(1)}, bf16[8,3584]{1,0:T(8,128)(2,1)S(1)}, u32[]{:S(2)}, u32[]{:S(2)}) collective-permute-start(bf16[8,3584]{1,0:T(8,128)(2,1)S(1)} %pad_maximum_fusion.2), channel_id=1, source_target_pairs={{0,16},{4,20},{8,24},{12,28},{16,0},{20,4},{24,8},{28,12},{1,17},{... | collective-permute-start | bytes 172040 | tf_op jit(solution)/shard_map/ppermute | solution.py:199
  9.9 6.0 %collective-permute-start.6 = (bf16[8,3584]{1,0:T(8,128)(2,1)S(1)}, bf16[8,3584]{1,0:T(8,128)(2,1)S(1)}, u32[]{:S(2)}, u32[]{:S(2)}) collective-permute-start(bf16[8,3584]{1,0:T(8,128)(2,1)S(1)} %pad_maximum_fusion.3), channel_id=1, source_target_pairs={{0,24},{4,28},{8,16},{12,20},{16,8},{20,12},{24,0},{28,4},{1,25},{... | collective-permute-start | bytes 172040 | tf_op jit(solution)/shard_map/ppermute | solution.py:199
  10.1 8.9 %collective-permute-start.4 = (bf16[16,3584]{1,0:T(8,128)(2,1)S(1)}, bf16[16,3584]{1,0:T(8,128)(2,1)S(1)}, u32[]{:S(2)}, u32[]{:S(2)}) collective-permute-start(bf16[16,3584]{1,0:T(8,128)(2,1)S(1)} %pad_maximum_fusion.near_ref.refs_0_), channel_id=1, source_target_pairs={{0,3},{1,2},{2,1},{3,0},{4,7},{5,6},{6,5},{7,4},{8,11},{9,10},{10,... | collective-permute-start | bytes 344072 | tf_op jit(solution)/shard_map/ppermute | solution.py:199
  12.8 6.8 %collective-permute-start.3 = (bf16[16,3584]{1,0:T(8,128)(2,1)S(1)}, bf16[16,3584]{1,0:T(8,128)(2,1)S(1)}, u32[]{:S(2)}, u32[]{:S(2)}) collective-permute-start(bf16[16,3584]{1,0:T(8,128)(2,1)S(1)} %pad_maximum_fusion.near_ref.refs_0_), channel_id=1, source_target_pairs={{0,2},{1,3},{2,0},{3,1},{4,6},{5,7},{6,4},{7,5},{8,10},{9,11},{10,... | collective-permute-start | bytes 344072 | tf_op jit(solution)/shard_map/ppermute | solution.py:199
  13.3 6.3 %collective-permute-start.2 = (bf16[16,3584]{1,0:T(8,128)(2,1)S(1)}, bf16[16,3584]{1,0:T(8,128)(2,1)S(1)}, u32[]{:S(2)}, u32[]{:S(2)}) collective-permute-start(bf16[16,3584]{1,0:T(8,128)(2,1)S(1)} %pad_maximum_fusion.near_ref.refs_0_), channel_id=1, source_target_pairs={{0,1},{1,0},{2,3},{3,2},{4,5},{5,4},{6,7},{7,6},{8,9},{9,8},{10,11... | collective-permute-start | bytes 344072 | tf_op jit(solution)/shard_map/ppermute | solution.py:199
  16.0 7.0 %collective-permute-start.9 = (bf16[16,3584]{1,0:T(8,128)(2,1)S(1)}, bf16[16,3584]{1,0:T(8,128)(2,1)S(1)}, u32[]{:S(2)}, u32[]{:S(2)}) collective-permute-start(bf16[16,3584]{1,0:T(8,128)(2,1)S(1)} %shard_map.95.refs_4_), channel_id=1, source_target_pairs={{0,3},{1,2},{2,1},{3,0},{4,7},{5,6},{6,5},{7,4},{8,11},{9,10},{10,... | collective-permute-start | bytes 344072 | tf_op jit(solution)/shard_map/ppermute | solution.py:199
  18.5 5.2 %collective-permute-start.8 = (bf16[16,3584]{1,0:T(8,128)(2,1)S(1)}, bf16[16,3584]{1,0:T(8,128)(2,1)S(1)}, u32[]{:S(2)}, u32[]{:S(2)}) collective-permute-start(bf16[16,3584]{1,0:T(8,128)(2,1)S(1)} %shard_map.95.refs_4_), channel_id=1, source_target_pairs={{0,2},{1,3},{2,0},{3,1},{4,6},{5,7},{6,4},{7,5},{8,10},{9,11},{10,... | collective-permute-start | bytes 344072 | tf_op jit(solution)/shard_map/ppermute | solution.py:199
  19.0 4.8 %collective-permute-start.7 = (bf16[16,3584]{1,0:T(8,128)(2,1)S(1)}, bf16[16,3584]{1,0:T(8,128)(2,1)S(1)}, u32[]{:S(2)}, u32[]{:S(2)}) collective-permute-start(bf16[16,3584]{1,0:T(8,128)(2,1)S(1)} %shard_map.95.refs_4_), channel_id=1, source_target_pairs={{0,1},{1,0},{2,3},{3,2},{4,5},{5,4},{6,7},{7,6},{8,9},{9,8},{10,11... | collective-permute-start | bytes 344072 | tf_op jit(solution)/shard_map/ppermute | solution.py:199

commit v4 on v3

--- a/solution.py
+++ b/solution.py
@@ -74,7 +74,7 @@
 def pick_rows(experts, ids, probs, tokens, out_grad):
     top = ids.shape[0]
     count, channels = tokens.shape
-    pieces = 4
+    pieces = 2
     shape = pltpu.VMEM((experts * ROWS // 2, channels), jnp.bfloat16)
     return pl.pallas_call(
         pick_kernel,
@@ -119,31 +119,49 @@
     )(*after, *in_hbm(w_gate, w_up, w_down))
 
 
-def join_kernel(first_ref, second_ref, near_ref, out_ref):
-    half = first_ref.shape[0]
-    out_ref[:half] = first_ref[...]
-    out_ref[half:] = second_ref[...]
-
-
-def join(first, second, near):
+def deal_kernel(own_ref, other_ref, *blocks):
+    for place, block in enumerate(blocks):
+        cut = slice(place * ROWS, (place + 1) * ROWS)
+        block[:ROWS] = own_ref[cut]
+        block[ROWS:] = other_ref[cut]
+
+
+def deal(own, other):
+    places = own.shape[0] // ROWS
+    return pl.pallas_call(
+        deal_kernel,
+        out_shape=[pltpu.VMEM((2 * ROWS, own.shape[1]), own.dtype)] * places,
+        in_specs=[VMEM, VMEM],
+        out_specs=[VMEM] * places,
+        compiler_params=pltpu.CompilerParams(vmem_limit_bytes=8 * MIB),
+    )(own, other)
+
+
+def join_kernel(first_ref, *refs):
+    *_, out_ref = refs
+    pieces = (first_ref,) + refs[: out_ref.shape[0] // first_ref.shape[0] - 1]
+    size = first_ref.shape[0]
+    for place, piece in enumerate(pieces):
+        out_ref[place * size : (place + 1) * size] = piece[...]
+
+
+def join(pieces, after=(), flops=0):
+    size, channels = pieces[0].shape
     return pl.pallas_call(
         join_kernel,
-        out_shape=pltpu.VMEM((2 * first.shape[0], first.shape[1]), first.dtype),
-        in_specs=[VMEM, VMEM, pl.BlockSpec(memory_space=pl.ANY)],
+        out_shape=pltpu.VMEM((len(pieces) * size, channels), pieces[0].dtype),
+        in_specs=[VMEM] * len(pieces) + [pl.BlockSpec(memory_space=pl.ANY)] * len(after),
         out_specs=VMEM,
-        compiler_params=pltpu.CompilerParams(vmem_limit_bytes=4 * MIB),
-        cost_estimate=pl.CostEstimate(flops=10**9, bytes_accessed=0, transcendentals=0),
-    )(first, second, near)
+        compiler_params=pltpu.CompilerParams(vmem_limit_bytes=8 * MIB),
+        cost_estimate=pl.CostEstimate(flops=flops, bytes_accessed=0, transcendentals=0),
+    )(*pieces, *after)
 
 
 def grads_kernel(pieces_in, *refs):
     parts = refs[:pieces_in]
     gate_ref, up_ref, down_ref, out_gate, out_up, out_down, rows_ref, buf, sems = refs[pieces_in:]
-    start = 0
-    for part in parts:
-        rows_ref[pl.ds(start, part.shape[0])] = part[...]
-        start += part.shape[0]
-    rows = rows_ref[...]
+    rows = jnp.concatenate([part[...] for part in parts], axis=0)
+    rows_ref[...] = rows
     count, channels = rows.shape
     contract = (((1,), (1,)), ((), ()))
     gate_pre = lax.dot_general(gate_ref[...], rows, contract, preferred_element_type=jnp.float32)
@@ -208,18 +226,12 @@
 
 def local(tokens, expert_ids, gate_probs, out_grad, w_gate, w_up, w_down):
     experts = w_gate.shape[0] * lax.axis_size("expert")
-    places = experts // 2
+    near_places = experts // 4
     own, other = pick_rows(experts, expert_ids.T, gate_probs.T, tokens, out_grad)
-    other = swap(other, "expert", 1)
-    blocks = []
-    for place in range(places):
-        cut = slice(place * ROWS, (place + 1) * ROWS)
-        blocks.append(jnp.concatenate([own[cut], other[cut]]))
-    arrived = [blocks[0]] + [swap(blocks[place], "expert", 2 * place) for place in range(1, places)]
-    near = jnp.concatenate(arrived[: places // 2])
-    middle = places // 4
-    far = [jnp.concatenate(arrived[places // 2 :][:middle]), jnp.concatenate(arrived[places // 2 :][middle:])]
-    far = join(far[0], far[1], near)
+    blocks = deal(own, swap(other, "expert", 1))
+    arrived = [swap(block, "expert", 2 * place) if place else block for place, block in enumerate(blocks)]
+    near = join(arrived[:near_places], flops=0)
+    far = join(arrived[near_places:], after=(near,), flops=10**9)
     parts = spread(near)
     gate, up, down = load_weights(parts + [far], w_gate[0], w_up[0], w_down[0])
     parts = parts + spread(far)

time: 28.2 us -> 27.8 us (0.986)
  transfers between devices with their start and end apart: 10 -> 10, of which waited for: 5 -> 6; matrix products, arithmetic and copies ran while one was open for 1% -> 0% of each run, Pallas kernels for 9% -> 10%
where the time goes in v4:
time: 27.8 us; the launch traced here: 27.6 us
  starting transfers between devices  13.2 us (47%)
  Pallas kernels  8.75 us (31%)
  waiting for transfers between devices  5.01 us (18%)
  between operations  0.67 us (2%)
    ppermute x10, starting transfers between devices, swap(): lax.ppermute(rows, axis, [(place, place ^ bits) for place in range(count)])  13.2 us
    ppermute x10, waiting for transfers between devices, swap(): lax.ppermute(rows, axis, [(place, place ^ bits) for place in range(count)])  5.01 us
    pallas_call x1, Pallas kernels, weight_grads(): pl.pallas_call(functools.partial(grads_kernel, len(parts)), out_shape=(sh...  4.26 us
    pallas_call x1, Pallas kernels, load_weights(): pl.pallas_call(load_kernel, out_shape=(shape, shape, shape), in_specs=[pl...  2.61 us
    pallas_call x1, Pallas kernels, pick_rows(): pl.pallas_call(pick_kernel, out_shape=(shape, shape), in_specs=[HBM] * 4,...  1.82 us
  transfers between devices with their start and end apart: 10, of which 6 were waited for; matrix products, arithmetic and copies ran while one was open for 0% of the time, Pallas kernels for 10%

profile of v4, /device:TPU:0, one launch (start us, length us, event | category | flops | bytes accessed | tf_op | source)
XLA Modules:
  0.0 27.6 jit_solution(4361779286622037025)
XLA Ops:
  0.6 1.8 %shard_map.94 = (bf16[16,3584]{1,0:T(8,128)(2,1)S(1)}, bf16[16,3584]{1,0:T(8,128)(2,1)S(1)}) custom-call(s32[8,128]{1,0:T(8,128)} %bitcast.11, f32[8,128]{1,0:T(8,128)} %bitcast.12, bf16[128,3584]{1,0:T(8,128)(2,1)} %tokens_hbm.1, bf16[128,3584]{1,0:T(8,128)(2,1)} %grad_hbm.1), custom_call_target="tpu_custom_call" | custom-call | tf_op jit(solution)/shard_map/pallas_call | solution.py:79
  2.5 0.5 %collective-permute-start = (bf16[16,3584]{1,0:T(8,128)(2,1)S(1)}, bf16[16,3584]{1,0:T(8,128)(2,1)S(1)}, u32[]{:S(2)}, u32[]{:S(2)}) collective-permute-start(bf16[16,3584]{1,0:T(8,128)(2,1)S(1)} %get-tuple-element.16), channel_id=1, source_target_pairs={{0,4},{4,0},{8,12},{12,8},{16,20},{20,16},{24,28},{28,24},{1,5},{5... | collective-permute-start | bytes 344072 | tf_op jit(solution)/shard_map/ppermute | solution.py:217
  3.0 1.0 %collective-permute-done.other_ref = bf16[16,3584]{1,0:T(8,128)(2,1)S(1)} collective-permute-done((bf16[16,3584]{1,0:T(8,128)(2,1)S(1)}, bf16[16,3584]{1,0:T(8,128)(2,1)S(1)}, u32[]{:S(2)}, u32[]{:S(2)}) %collective-permute-start) | collective-permute-done | bytes 114720 | tf_op jit(solution)/shard_map/ppermute | solution.py:217
  4.0 3.0 %collective-permute-start.1 = (bf16[8,3584]{1,0:T(8,128)(2,1)S(1)}, bf16[8,3584]{1,0:T(8,128)(2,1)S(1)}, u32[]{:S(2)}, u32[]{:S(2)}) collective-permute-start(bf16[8,3584]{1,0:T(8,128)(2,1)S(1)} %get-tuple-element.18), channel_id=1, source_target_pairs={{0,8},{4,12},{8,0},{12,4},{16,24},{20,28},{24,16},{28,20},{1,9},{5... | collective-permute-start | bytes 172040 | tf_op jit(solution)/shard_map/ppermute | solution.py:217
  7.0 2.6 %collective-permute-start.5 = (bf16[8,3584]{1,0:T(8,128)(2,1)S(1)}, bf16[8,3584]{1,0:T(8,128)(2,1)S(1)}, u32[]{:S(2)}, u32[]{:S(2)}) collective-permute-start(bf16[8,3584]{1,0:T(8,128)(2,1)S(1)} %get-tuple-element.19), channel_id=1, source_target_pairs={{0,16},{4,20},{8,24},{12,28},{16,0},{20,4},{24,8},{28,12},{1,17},{... | collective-permute-start | bytes 172040 | tf_op jit(solution)/shard_map/ppermute | solution.py:217
  9.6 0.0 collective-permute-start.6
  9.6 0.0 collective-permute-done.1.refs_0_
  9.6 2.7 %collective-permute-start.4 = (bf16[16,3584]{1,0:T(8,128)(2,1)S(1)}, bf16[16,3584]{1,0:T(8,128)(2,1)S(1)}, u32[]{:S(2)}, u32[]{:S(2)}) collective-permute-start(bf16[16,3584]{1,0:T(8,128)(2,1)S(1)} %shard_map.96.refs_1_.refs_0_), channel_id=1, source_target_pairs={{0,3},{1,2},{2,1},{3,0},{4,7},{5,6},{6,5},{7,4},{8,11},{9,10},{10,... | collective-permute-start | bytes 344072 | tf_op jit(solution)/shard_map/ppermute | solution.py:217
  12.3 0.5 %collective-permute-start.3 = (bf16[16,3584]{1,0:T(8,128)(2,1)S(1)}, bf16[16,3584]{1,0:T(8,128)(2,1)S(1)}, u32[]{:S(2)}, u32[]{:S(2)}) collective-permute-start(bf16[16,3584]{1,0:T(8,128)(2,1)S(1)} %shard_map.96.refs_1_.refs_0_), channel_id=1, source_target_pairs={{0,2},{1,3},{2,0},{3,1},{4,6},{5,7},{6,4},{7,5},{8,10},{9,11},{10,... | collective-permute-start | bytes 344072 | tf_op jit(solution)/shard_map/ppermute | solution.py:217
  12.8 0.3 %collective-permute-start.2 = (bf16[16,3584]{1,0:T(8,128)(2,1)S(1)}, bf16[16,3584]{1,0:T(8,128)(2,1)S(1)}, u32[]{:S(2)}, u32[]{:S(2)}) collective-permute-start(bf16[16,3584]{1,0:T(8,128)(2,1)S(1)} %shard_map.96.refs_1_.refs_0_), channel_id=1, source_target_pairs={{0,1},{1,0},{2,3},{3,2},{4,5},{5,4},{6,7},{7,6},{8,9},{9,8},{10,11... | collective-permute-start | bytes 344072 | tf_op jit(solution)/shard_map/ppermute | solution.py:217
  13.1 0.2 collective-permute-done.5.first_ref
  13.4 2.2 %collective-permute-done.6.refs_0_ = bf16[8,3584]{1,0:T(8,128)(2,1)S(1)} collective-permute-done((bf16[8,3584]{1,0:T(8,128)(2,1)S(1)}, bf16[8,3584]{1,0:T(8,128)(2,1)S(1)}, u32[]{:S(2)}, u32[]{:S(2)}) %collective-permute-start.6) | collective-permute-done | bytes 57376 | tf_op jit(solution)/shard_map/ppermute | solution.py:217
  15.6 2.5 %collective-permute-start.9 = (bf16[16,3584]{1,0:T(8,128)(2,1)S(1)}, bf16[16,3584]{1,0:T(8,128)(2,1)S(1)}, u32[]{:S(2)}, u32[]{:S(2)}) collective-permute-start(bf16[16,3584]{1,0:T(8,128)(2,1)S(1)} %shard_map.97.refs_4_), channel_id=1, source_target_pairs={{0,3},{1,2},{2,1},{3,0},{4,7},{5,6},{6,5},{7,4},{8,11},{9,10},{10,... | collective-permute-start | bytes 344072 | tf_op jit(solution)/shard_map/ppermute | solution.py:217
  18.1 0.5 %collective-permute-start.8 = (bf16[16,3584]{1,0:T(8,128)(2,1)S(1)}, bf16[16,3584]{1,0:T(8,128)(2,1)S(1)}, u32[]{:S(2)}, u32[]{:S(2)}) collective-permute-start(bf16[16,3584]{1,0:T(8,128)(2,1)S(1)} %shard_map.97.refs_4_), channel_id=1, source_target_pairs={{0,2},{1,3},{2,0},{3,1},{4,6},{5,7},{6,4},{7,5},{8,10},{9,11},{10,... | collective-permute-start | bytes 344072 | tf_op jit(solution)/shard_map/ppermute | solution.py:217
  18.6 0.0 collective-permute-done.4.refs_3_
  18.6 0.5 %collective-permute-start.7 = (bf16[16,3584]{1,0:T(8,128)(2,1)S(1)}, bf16[16,3584]{1,0:T(8,128)(2,1)S(1)}, u32[]{:S(2)}, u32[]{:S(2)}) collective-permute-start(bf16[16,3584]{1,0:T(8,128)(2,1)S(1)} %shard_map.97.refs_4_), channel_id=1, source_target_pairs={{0,1},{1,0},{2,3},{3,2},{4,5},{5,4},{6,7},{7,6},{8,9},{9,8},{10,11... | collective-permute-start | bytes 344072 | tf_op jit(solution)/shard_map/ppermute | solution.py:217
  19.1 0.0 collective-permute-done.3.refs_2_
  19.1 0.0 collective-permute-done.2.refs_1_
  19.1 2.6 %shard_map.98 = (bf16[256,3584]{1,0:T(8,128)(2,1)S(1)}, bf16[256,3584]{1,0:T(8,128)(2,1)S(1)}, bf16[256,3584]{1,0:T(8,128)(2,1)S(1)}) custom-call(bf16[16,3584]{1,0:T(8,128)(2,1)S(1)} %shard_map.96.refs_1_.refs_0_, bf16[16,3584]{1,0:T(8,128)(2,1)S(1)} %collective-permute-done.2.refs_1_, bf16[16,3584]{1,0:T(8,128)(2,1)S(1)} %collective-permute-done.3.refs_2_, ...), custom_call_target="tpu_custom_call" | custom-call | bytes 11010048 | tf_op jit(solution)/shard_map/pallas_call | solution.py:111
  21.7 0.8 %collective-permute-done.9.refs_7_ = bf16[16,3584]{1,0:T(8,128)(2,1)S(1)} collective-permute-done((bf16[16,3584]{1,0:T(8,128)(2,1)S(1)}, bf16[16,3584]{1,0:T(8,128)(2,1)S(1)}, u32[]{:S(2)}, u32[]{:S(2)}) %collective-permute-start.9) | collective-permute-done | bytes 114720 | tf_op jit(solution)/shard_map/ppermute | solution.py:217
  22.5 0.8 %collective-permute-done.8.refs_6_ = bf16[16,3584]{1,0:T(8,128)(2,1)S(1)} collective-permute-done((bf16[16,3584]{1,0:T(8,128)(2,1)S(1)}, bf16[16,3584]{1,0:T(8,128)(2,1)S(1)}, u32[]{:S(2)}, u32[]{:S(2)}) %collective-permute-start.8) | collective-permute-done | bytes 114720 | tf_op jit(solution)/shard_map/ppermute | solution.py:217
  23.3 0.1 collective-permute-done.7.refs_5_
  23.4 4.3 %shard_map.99 = (bf16[256,3584]{1,0:T(8,128)(2,1)}, bf16[256,3584]{1,0:T(8,128)(2,1)}, bf16[256,3584]{1,0:T(8,128)(2,1)}) custom-call(bf16[16,3584]{1,0:T(8,128)(2,1)S(1)} %shard_map.96.refs_1_.refs_0_, bf16[16,3584]{1,0:T(8,128)(2,1)S(1)} %collective-permute-done.2.refs_1_, bf16[16,3584]{1,0:T(8,128)(2,1)S(1)} %collective-permute-done.3.refs_2_, ...), custom_call_target="tpu_custom_call" | custom-call | tf_op jit(solution)/shard_map/pallas_call | solution.py:201
  (3 shorter events, 0.1 us)
Async XLA Ops:
  2.5 1.5 %collective-permute-start = (bf16[16,3584]{1,0:T(8,128)(2,1)S(1)}, bf16[16,3584]{1,0:T(8,128)(2,1)S(1)}, u32[]{:S(2)}, u32[]{:S(2)}) collective-permute-start(bf16[16,3584]{1,0:T(8,128)(2,1)S(1)} %get-tuple-element.16), channel_id=1, source_target_pairs={{0,4},{4,0},{8,12},{12,8},{16,20},{20,16},{24,28},{28,24},{1,5},{5... | collective-permute-start | bytes 344072 | tf_op jit(solution)/shard_map/ppermute | solution.py:217
  4.0 5.6 %collective-permute-start.1 = (bf16[8,3584]{1,0:T(8,128)(2,1)S(1)}, bf16[8,3584]{1,0:T(8,128)(2,1)S(1)}, u32[]{:S(2)}, u32[]{:S(2)}) collective-permute-start(bf16[8,3584]{1,0:T(8,128)(2,1)S(1)} %get-tuple-element.18), channel_id=1, source_target_pairs={{0,8},{4,12},{8,0},{12,4},{16,24},{20,28},{24,16},{28,20},{1,9},{5... | collective-permute-start | bytes 172040 | tf_op jit(solution)/shard_map/ppermute | solution.py:217
  7.0 6.4 %collective-permute-start.5 = (bf16[8,3584]{1,0:T(8,128)(2,1)S(1)}, bf16[8,3584]{1,0:T(8,128)(2,1)S(1)}, u32[]{:S(2)}, u32[]{:S(2)}) collective-permute-start(bf16[8,3584]{1,0:T(8,128)(2,1)S(1)} %get-tuple-element.19), channel_id=1, source_target_pairs={{0,16},{4,20},{8,24},{12,28},{16,0},{20,4},{24,8},{28,12},{1,17},{... | collective-permute-start | bytes 172040 | tf_op jit(solution)/shard_map/ppermute | solution.py:217
  9.6 6.0 %collective-permute-start.6 = (bf16[8,3584]{1,0:T(8,128)(2,1)S(1)}, bf16[8,3584]{1,0:T(8,128)(2,1)S(1)}, u32[]{:S(2)}, u32[]{:S(2)}) collective-permute-start(bf16[8,3584]{1,0:T(8,128)(2,1)S(1)} %get-tuple-element.20), channel_id=1, source_target_pairs={{0,24},{4,28},{8,16},{12,20},{16,8},{20,12},{24,0},{28,4},{1,25},{... | collective-permute-start | bytes 172040 | tf_op jit(solution)/shard_map/ppermute | solution.py:217
  9.6 9.0 %collective-permute-start.4 = (bf16[16,3584]{1,0:T(8,128)(2,1)S(1)}, bf16[16,3584]{1,0:T(8,128)(2,1)S(1)}, u32[]{:S(2)}, u32[]{:S(2)}) collective-permute-start(bf16[16,3584]{1,0:T(8,128)(2,1)S(1)} %shard_map.96.refs_1_.refs_0_), channel_id=1, source_target_pairs={{0,3},{1,2},{2,1},{3,0},{4,7},{5,6},{6,5},{7,4},{8,11},{9,10},{10,... | collective-permute-start | bytes 344072 | tf_op jit(solution)/shard_map/ppermute | solution.py:217
  12.3 6.8 %collective-permute-start.3 = (bf16[16,3584]{1,0:T(8,128)(2,1)S(1)}, bf16[16,3584]{1,0:T(8,128)(2,1)S(1)}, u32[]{:S(2)}, u32[]{:S(2)}) collective-permute-start(bf16[16,3584]{1,0:T(8,128)(2,1)S(1)} %shard_map.96.refs_1_.refs_0_), channel_id=1, source_target_pairs={{0,2},{1,3},{2,0},{3,1},{4,6},{5,7},{6,4},{7,5},{8,10},{9,11},{10,... | collective-permute-start | bytes 344072 | tf_op jit(solution)/shard_map/ppermute | solution.py:217
  12.8 6.3 %collective-permute-start.2 = (bf16[16,3584]{1,0:T(8,128)(2,1)S(1)}, bf16[16,3584]{1,0:T(8,128)(2,1)S(1)}, u32[]{:S(2)}, u32[]{:S(2)}) collective-permute-start(bf16[16,3584]{1,0:T(8,128)(2,1)S(1)} %shard_map.96.refs_1_.refs_0_), channel_id=1, source_target_pairs={{0,1},{1,0},{2,3},{3,2},{4,5},{5,4},{6,7},{7,6},{8,9},{9,8},{10,11... | collective-permute-start | bytes 344072 | tf_op jit(solution)/shard_map/ppermute | solution.py:217
  15.6 6.9 %collective-permute-start.9 = (bf16[16,3584]{1,0:T(8,128)(2,1)S(1)}, bf16[16,3584]{1,0:T(8,128)(2,1)S(1)}, u32[]{:S(2)}, u32[]{:S(2)}) collective-permute-start(bf16[16,3584]{1,0:T(8,128)(2,1)S(1)} %shard_map.97.refs_4_), channel_id=1, source_target_pairs={{0,3},{1,2},{2,1},{3,0},{4,7},{5,6},{6,5},{7,4},{8,11},{9,10},{10,... | collective-permute-start | bytes 344072 | tf_op jit(solution)/shard_map/ppermute | solution.py:217
  18.1 5.2 %collective-permute-start.8 = (bf16[16,3584]{1,0:T(8,128)(2,1)S(1)}, bf16[16,3584]{1,0:T(8,128)(2,1)S(1)}, u32[]{:S(2)}, u32[]{:S(2)}) collective-permute-start(bf16[16,3584]{1,0:T(8,128)(2,1)S(1)} %shard_map.97.refs_4_), channel_id=1, source_target_pairs={{0,2},{1,3},{2,0},{3,1},{4,6},{5,7},{6,4},{7,5},{8,10},{9,11},{10,... | collective-permute-start | bytes 344072 | tf_op jit(solution)/shard_map/ppermute | solution.py:217
  18.6 4.8 %collective-permute-start.7 = (bf16[16,3584]{1,0:T(8,128)(2,1)S(1)}, bf16[16,3584]{1,0:T(8,128)(2,1)S(1)}, u32[]{:S(2)}, u32[]{:S(2)}) collective-permute-start(bf16[16,3584]{1,0:T(8,128)(2,1)S(1)} %shard_map.97.refs_4_), channel_id=1, source_target_pairs={{0,1},{1,0},{2,3},{3,2},{4,5},{5,4},{6,7},{7,6},{8,9},{9,8},{10,11... | collective-permute-start | bytes 344072 | tf_op jit(solution)/shard_map/ppermute | solution.py:217

commit v5 on v4

--- a/solution.py
+++ b/solution.py
@@ -41,8 +41,10 @@
     row = lax.broadcasted_iota(jnp.int32, (total, 1), 0)
     block = row // ROWS
     places = total // ROWS // 2
-    relative = 2 * (block % places) + block // places
-    expert = lax.axis_index("expert") ^ relative
+    place, other = block % places, block // places
+    me = lax.axis_index("expert")
+    along = jnp.where(2 * place >= places, place ^ ((me ^ other ^ 1) & 1), place)
+    expert = me ^ (2 * along + other)
     slot = (row % CAP).astype(jnp.float32)
     is_x = row % ROWS < CAP
     earlier = (
@@ -217,11 +219,22 @@
     return lax.ppermute(rows, axis, [(place, place ^ bits) for place in range(count)])
 
 
+def swap_by_core(rows, bits):
+    experts, count = lax.axis_size("expert"), lax.axis_size("dp")
+    pairs = []
+    for expert in range(experts):
+        for place in range(count):
+            pairs.append((expert * count + place, expert * count + (place ^ bits[expert % 2])))
+    return lax.ppermute(rows, ("expert", "dp"), pairs)
+
+
 def spread(rows):
     count = lax.axis_size("dp")
     if count > 4:
         return [lax.all_gather(rows, "dp", axis=0, tiled=True)]
-    return [rows] + [swap(rows, "dp", bits) for bits in range(1, count)]
+    if count < 4:
+        return [rows] + [swap(rows, "dp", bits) for bits in range(1, count)]
+    return [rows, swap_by_core(rows, (1, 2)), swap_by_core(rows, (2, 1)), swap(rows, "dp", 3)]
 
 
 def local(tokens, expert_ids, gate_probs, out_grad, w_gate, w_up, w_down):
@@ -229,7 +242,11 @@
     near_places = experts // 4
     own, other = pick_rows(experts, expert_ids.T, gate_probs.T, tokens, out_grad)
     blocks = deal(own, swap(other, "expert", 1))
-    arrived = [swap(block, "expert", 2 * place) if place else block for place, block in enumerate(blocks)]
+    arrived = []
+    for place, block in enumerate(blocks):
+        along = [place ^ 1, place] if place >= near_places else [place, place]
+        pairs = [(expert, expert ^ (2 * along[expert % 2])) for expert in range(experts)]
+        arrived.append(lax.ppermute(block, "expert", pairs) if place else block)
     near = join(arrived[:near_places], flops=0)
     far = join(arrived[near_places:], after=(near,), flops=10**9)
     parts = spread(near)

time: 27.8 us -> 27.7 us (level)
    ppermute x0 -> x7, starting transfers between devices: none -> 7.66 us  [the longest x3 5.59 us: local(): arrived.append(lax.ppermute(block, 'expert', pairs) if place else block)]
    ppermute x10 -> x3, starting transfers between devices: 13.2 us -> 5.55 us  [swap(): lax.ppermute(rows, axis, [(place, place ^ bits) for place in range(count)])]
    ppermute x10 -> x3, waiting for transfers between devices: 5.01 us -> 1.47 us  [swap(): lax.ppermute(rows, axis, [(place, place ^ bits) for place in range(count)])]
    ppermute x0 -> x7, waiting for transfers between devices: none -> 3.45 us  [the longest x3 2.25 us: local(): arrived.append(lax.ppermute(block, 'expert', pairs) if place else block)]
  transfers between devices with their start and end apart: 10 -> 10, of which waited for: 6 -> 4; matrix products, arithmetic and copies ran while one was open for 0% -> 0% of each run, Pallas kernels for 10% -> 10%
where the time goes in v5:
time: 27.7 us; the launch traced here: 27.5 us
  starting transfers between devices  13.2 us (48%)
  Pallas kernels  8.75 us (32%)
  waiting for transfers between devices  4.91 us (18%)
  between operations  0.67 us (2%)
    ppermute x3, starting transfers between devices, local(): arrived.append(lax.ppermute(block, 'expert', pairs) if place else block)  5.59 us
    ppermute x3, starting transfers between devices, swap(): lax.ppermute(rows, axis, [(place, place ^ bits) for place in range(count)])  5.55 us
    pallas_call x1, Pallas kernels, weight_grads(): pl.pallas_call(functools.partial(grads_kernel, len(parts)), out_shape=(sh...  4.26 us
    pallas_call x1, Pallas kernels, load_weights(): pl.pallas_call(load_kernel, out_shape=(shape, shape, shape), in_specs=[pl...  2.61 us
    ppermute x3, waiting for transfers between devices, local(): arrived.append(lax.ppermute(block, 'expert', pairs) if place else block)  2.25 us
    ppermute x4, starting transfers between devices, swap_by_core(): return lax.ppermute(rows, ('expert', 'dp'), pairs)  2.07 us
    pallas_call x1, Pallas kernels, pick_rows(): pl.pallas_call(pick_kernel, out_shape=(shape, shape), in_specs=[HBM] * 4,...  1.82 us
    ppermute x3, waiting for transfers between devices, swap(): lax.ppermute(rows, axis, [(place, place ^ bits) for place in range(count)])  1.47 us
  transfers between devices with their start and end apart: 10, of which 4 were waited for; matrix products, arithmetic and copies ran while one was open for 0% of the time, Pallas kernels for 10%

profile of v5, /device:TPU:0, one launch (start us, length us, event | category | flops | bytes accessed | tf_op | source)
XLA Modules:
  0.0 27.5 jit_solution(12157378477079866786)
XLA Ops:
  0.6 1.8 %shard_map.94 = (bf16[16,3584]{1,0:T(8,128)(2,1)S(1)}, bf16[16,3584]{1,0:T(8,128)(2,1)S(1)}) custom-call(s32[8,128]{1,0:T(8,128)} %bitcast.11, f32[8,128]{1,0:T(8,128)} %bitcast.12, bf16[128,3584]{1,0:T(8,128)(2,1)} %tokens_hbm.1, bf16[128,3584]{1,0:T(8,128)(2,1)} %grad_hbm.1), custom_call_target="tpu_custom_call" | custom-call | tf_op jit(solution)/shard_map/pallas_call | solution.py:81
  2.5 0.5 %collective-permute-start = (bf16[16,3584]{1,0:T(8,128)(2,1)S(1)}, bf16[16,3584]{1,0:T(8,128)(2,1)S(1)}, u32[]{:S(2)}, u32[]{:S(2)}) collective-permute-start(bf16[16,3584]{1,0:T(8,128)(2,1)S(1)} %get-tuple-element.16), channel_id=1, source_target_pairs={{0,4},{4,0},{8,12},{12,8},{16,20},{20,16},{24,28},{28,24},{1,5},{5... | collective-permute-start | bytes 344072 | tf_op jit(solution)/shard_map/ppermute | solution.py:219
  3.0 1.0 %collective-permute-done.other_ref = bf16[16,3584]{1,0:T(8,128)(2,1)S(1)} collective-permute-done((bf16[16,3584]{1,0:T(8,128)(2,1)S(1)}, bf16[16,3584]{1,0:T(8,128)(2,1)S(1)}, u32[]{:S(2)}, u32[]{:S(2)}) %collective-permute-start) | collective-permute-done | bytes 114720 | tf_op jit(solution)/shard_map/ppermute | solution.py:219
  4.0 3.0 %collective-permute-start.1 = (bf16[8,3584]{1,0:T(8,128)(2,1)S(1)}, bf16[8,3584]{1,0:T(8,128)(2,1)S(1)}, u32[]{:S(2)}, u32[]{:S(2)}) collective-permute-start(bf16[8,3584]{1,0:T(8,128)(2,1)S(1)} %get-tuple-element.18), channel_id=1, source_target_pairs={{0,8},{4,12},{8,0},{12,4},{16,24},{20,28},{24,16},{28,20},{1,9},{5... | collective-permute-start | bytes 172040 | tf_op jit(solution)/shard_map/ppermute | solution.py:249
  7.0 2.5 %collective-permute-start.5 = (bf16[8,3584]{1,0:T(8,128)(2,1)S(1)}, bf16[8,3584]{1,0:T(8,128)(2,1)S(1)}, u32[]{:S(2)}, u32[]{:S(2)}) collective-permute-start(bf16[8,3584]{1,0:T(8,128)(2,1)S(1)} %get-tuple-element.19), channel_id=1, source_target_pairs={{0,24},{4,20},{8,16},{12,28},{16,8},{20,4},{24,0},{28,12},{1,25},{... | collective-permute-start | bytes 172040 | tf_op jit(solution)/shard_map/ppermute | solution.py:249
  9.5 0.1 collective-permute-start.6
  9.6 0.0 collective-permute-done.1.refs_0_
  9.6 2.5 %collective-permute-start.4 = (bf16[16,3584]{1,0:T(8,128)(2,1)S(1)}, bf16[16,3584]{1,0:T(8,128)(2,1)S(1)}, u32[]{:S(2)}, u32[]{:S(2)}) collective-permute-start(bf16[16,3584]{1,0:T(8,128)(2,1)S(1)} %shard_map.96.refs_1_.refs_0_), channel_id=1, source_target_pairs={{0,3},{1,2},{2,1},{3,0},{4,7},{5,6},{6,5},{7,4},{8,11},{9,10},{10,... | collective-permute-start | bytes 344072 | tf_op jit(solution)/shard_map/ppermute | solution.py:219
  12.1 0.5 %collective-permute-start.3 = (bf16[16,3584]{1,0:T(8,128)(2,1)S(1)}, bf16[16,3584]{1,0:T(8,128)(2,1)S(1)}, u32[]{:S(2)}, u32[]{:S(2)}) collective-permute-start(bf16[16,3584]{1,0:T(8,128)(2,1)S(1)} %shard_map.96.refs_1_.refs_0_), channel_id=1, source_target_pairs={{0,2},{1,3},{2,0},{3,1},{4,5},{5,4},{6,7},{7,6},{8,10},{9,11},{10,... | collective-permute-start | bytes 344072 | tf_op jit(solution)/shard_map/ppermute | solution.py:228
  12.6 0.5 %collective-permute-start.2 = (bf16[16,3584]{1,0:T(8,128)(2,1)S(1)}, bf16[16,3584]{1,0:T(8,128)(2,1)S(1)}, u32[]{:S(2)}, u32[]{:S(2)}) collective-permute-start(bf16[16,3584]{1,0:T(8,128)(2,1)S(1)} %shard_map.96.refs_1_.refs_0_), channel_id=1, source_target_pairs={{0,1},{1,0},{2,3},{3,2},{4,6},{5,7},{6,4},{7,5},{8,9},{9,8},{10,11... | collective-permute-start | bytes 344072 | tf_op jit(solution)/shard_map/ppermute | solution.py:228
  13.1 0.0 collective-permute-done.5.first_ref
  13.1 2.2 %collective-permute-done.6.refs_0_ = bf16[8,3584]{1,0:T(8,128)(2,1)S(1)} collective-permute-done((bf16[8,3584]{1,0:T(8,128)(2,1)S(1)}, bf16[8,3584]{1,0:T(8,128)(2,1)S(1)}, u32[]{:S(2)}, u32[]{:S(2)}) %collective-permute-start.6) | collective-permute-done | bytes 57376 | tf_op jit(solution)/shard_map/ppermute | solution.py:249
  15.4 2.5 %collective-permute-start.9 = (bf16[16,3584]{1,0:T(8,128)(2,1)S(1)}, bf16[16,3584]{1,0:T(8,128)(2,1)S(1)}, u32[]{:S(2)}, u32[]{:S(2)}) collective-permute-start(bf16[16,3584]{1,0:T(8,128)(2,1)S(1)} %shard_map.97.refs_4_), channel_id=1, source_target_pairs={{0,3},{1,2},{2,1},{3,0},{4,7},{5,6},{6,5},{7,4},{8,11},{9,10},{10,... | collective-permute-start | bytes 344072 | tf_op jit(solution)/shard_map/ppermute | solution.py:219
  17.9 0.5 %collective-permute-start.8 = (bf16[16,3584]{1,0:T(8,128)(2,1)S(1)}, bf16[16,3584]{1,0:T(8,128)(2,1)S(1)}, u32[]{:S(2)}, u32[]{:S(2)}) collective-permute-start(bf16[16,3584]{1,0:T(8,128)(2,1)S(1)} %shard_map.97.refs_4_), channel_id=1, source_target_pairs={{0,2},{1,3},{2,0},{3,1},{4,5},{5,4},{6,7},{7,6},{8,10},{9,11},{10,... | collective-permute-start | bytes 344072 | tf_op jit(solution)/shard_map/ppermute | solution.py:228
  18.4 0.0 collective-permute-done.4.refs_3_
  18.4 0.5 %collective-permute-start.7 = (bf16[16,3584]{1,0:T(8,128)(2,1)S(1)}, bf16[16,3584]{1,0:T(8,128)(2,1)S(1)}, u32[]{:S(2)}, u32[]{:S(2)}) collective-permute-start(bf16[16,3584]{1,0:T(8,128)(2,1)S(1)} %shard_map.97.refs_4_), channel_id=1, source_target_pairs={{0,1},{1,0},{2,3},{3,2},{4,6},{5,7},{6,4},{7,5},{8,9},{9,8},{10,11... | collective-permute-start | bytes 344072 | tf_op jit(solution)/shard_map/ppermute | solution.py:228
  19.0 0.0 collective-permute-done.3.refs_2_
  19.0 0.0 collective-permute-done.2.refs_1_
  19.0 2.6 %shard_map.98 = (bf16[256,3584]{1,0:T(8,128)(2,1)S(1)}, bf16[256,3584]{1,0:T(8,128)(2,1)S(1)}, bf16[256,3584]{1,0:T(8,128)(2,1)S(1)}) custom-call(bf16[16,3584]{1,0:T(8,128)(2,1)S(1)} %shard_map.96.refs_1_.refs_0_, bf16[16,3584]{1,0:T(8,128)(2,1)S(1)} %collective-permute-done.2.refs_1_, bf16[16,3584]{1,0:T(8,128)(2,1)S(1)} %collective-permute-done.3.refs_2_, ...), custom_call_target="tpu_custom_call" | custom-call | bytes 11010048 | tf_op jit(solution)/shard_map/pallas_call | solution.py:113
  21.6 0.5 %collective-permute-done.9.refs_7_ = bf16[16,3584]{1,0:T(8,128)(2,1)S(1)} collective-permute-done((bf16[16,3584]{1,0:T(8,128)(2,1)S(1)}, bf16[16,3584]{1,0:T(8,128)(2,1)S(1)}, u32[]{:S(2)}, u32[]{:S(2)}) %collective-permute-start.9) | collective-permute-done | bytes 114720 | tf_op jit(solution)/shard_map/ppermute | solution.py:219
  22.1 1.2 %collective-permute-done.8.refs_6_ = bf16[16,3584]{1,0:T(8,128)(2,1)S(1)} collective-permute-done((bf16[16,3584]{1,0:T(8,128)(2,1)S(1)}, bf16[16,3584]{1,0:T(8,128)(2,1)S(1)}, u32[]{:S(2)}, u32[]{:S(2)}) %collective-permute-start.8) | collective-permute-done | bytes 114720 | tf_op jit(solution)/shard_map/ppermute | solution.py:228
  23.3 0.0 collective-permute-done.7.refs_5_
  23.3 4.3 %shard_map.99 = (bf16[256,3584]{1,0:T(8,128)(2,1)}, bf16[256,3584]{1,0:T(8,128)(2,1)}, bf16[256,3584]{1,0:T(8,128)(2,1)}) custom-call(bf16[16,3584]{1,0:T(8,128)(2,1)S(1)} %shard_map.96.refs_1_.refs_0_, bf16[16,3584]{1,0:T(8,128)(2,1)S(1)} %collective-permute-done.2.refs_1_, bf16[16,3584]{1,0:T(8,128)(2,1)S(1)} %collective-permute-done.3.refs_2_, ...), custom_call_target="tpu_custom_call" | custom-call | tf_op jit(solution)/shard_map/pallas_call | solution.py:203
  (3 shorter events, 0.1 us)
Async XLA Ops:
  2.5 1.5 %collective-permute-start = (bf16[16,3584]{1,0:T(8,128)(2,1)S(1)}, bf16[16,3584]{1,0:T(8,128)(2,1)S(1)}, u32[]{:S(2)}, u32[]{:S(2)}) collective-permute-start(bf16[16,3584]{1,0:T(8,128)(2,1)S(1)} %get-tuple-element.16), channel_id=1, source_target_pairs={{0,4},{4,0},{8,12},{12,8},{16,20},{20,16},{24,28},{28,24},{1,5},{5... | collective-permute-start | bytes 344072 | tf_op jit(solution)/shard_map/ppermute | solution.py:219
  4.0 5.6 %collective-permute-start.1 = (bf16[8,3584]{1,0:T(8,128)(2,1)S(1)}, bf16[8,3584]{1,0:T(8,128)(2,1)S(1)}, u32[]{:S(2)}, u32[]{:S(2)}) collective-permute-start(bf16[8,3584]{1,0:T(8,128)(2,1)S(1)} %get-tuple-element.18), channel_id=1, source_target_pairs={{0,8},{4,12},{8,0},{12,4},{16,24},{20,28},{24,16},{28,20},{1,9},{5... | collective-permute-start | bytes 172040 | tf_op jit(solution)/shard_map/ppermute | solution.py:249
  7.0 6.2 %collective-permute-start.5 = (bf16[8,3584]{1,0:T(8,128)(2,1)S(1)}, bf16[8,3584]{1,0:T(8,128)(2,1)S(1)}, u32[]{:S(2)}, u32[]{:S(2)}) collective-permute-start(bf16[8,3584]{1,0:T(8,128)(2,1)S(1)} %get-tuple-element.19), channel_id=1, source_target_pairs={{0,24},{4,20},{8,16},{12,28},{16,8},{20,4},{24,0},{28,12},{1,25},{... | collective-permute-start | bytes 172040 | tf_op jit(solution)/shard_map/ppermute | solution.py:249
  9.5 5.9 %collective-permute-start.6 = (bf16[8,3584]{1,0:T(8,128)(2,1)S(1)}, bf16[8,3584]{1,0:T(8,128)(2,1)S(1)}, u32[]{:S(2)}, u32[]{:S(2)}) collective-permute-start(bf16[8,3584]{1,0:T(8,128)(2,1)S(1)} %get-tuple-element.20), channel_id=1, source_target_pairs={{0,16},{4,28},{8,24},{12,20},{16,0},{20,12},{24,8},{28,4},{1,17},{... | collective-permute-start | bytes 172040 | tf_op jit(solution)/shard_map/ppermute | solution.py:249
  9.6 8.8 %collective-permute-start.4 = (bf16[16,3584]{1,0:T(8,128)(2,1)S(1)}, bf16[16,3584]{1,0:T(8,128)(2,1)S(1)}, u32[]{:S(2)}, u32[]{:S(2)}) collective-permute-start(bf16[16,3584]{1,0:T(8,128)(2,1)S(1)} %shard_map.96.refs_1_.refs_0_), channel_id=1, source_target_pairs={{0,3},{1,2},{2,1},{3,0},{4,7},{5,6},{6,5},{7,4},{8,11},{9,10},{10,... | collective-permute-start | bytes 344072 | tf_op jit(solution)/shard_map/ppermute | solution.py:219
  12.1 6.9 %collective-permute-start.3 = (bf16[16,3584]{1,0:T(8,128)(2,1)S(1)}, bf16[16,3584]{1,0:T(8,128)(2,1)S(1)}, u32[]{:S(2)}, u32[]{:S(2)}) collective-permute-start(bf16[16,3584]{1,0:T(8,128)(2,1)S(1)} %shard_map.96.refs_1_.refs_0_), channel_id=1, source_target_pairs={{0,2},{1,3},{2,0},{3,1},{4,5},{5,4},{6,7},{7,6},{8,10},{9,11},{10,... | collective-permute-start | bytes 344072 | tf_op jit(solution)/shard_map/ppermute | solution.py:228
  12.6 6.4 %collective-permute-start.2 = (bf16[16,3584]{1,0:T(8,128)(2,1)S(1)}, bf16[16,3584]{1,0:T(8,128)(2,1)S(1)}, u32[]{:S(2)}, u32[]{:S(2)}) collective-permute-start(bf16[16,3584]{1,0:T(8,128)(2,1)S(1)} %shard_map.96.refs_1_.refs_0_), channel_id=1, source_target_pairs={{0,1},{1,0},{2,3},{3,2},{4,6},{5,7},{6,4},{7,5},{8,9},{9,8},{10,11... | collective-permute-start | bytes 344072 | tf_op jit(solution)/shard_map/ppermute | solution.py:228
  15.4 6.7 %collective-permute-start.9 = (bf16[16,3584]{1,0:T(8,128)(2,1)S(1)}, bf16[16,3584]{1,0:T(8,128)(2,1)S(1)}, u32[]{:S(2)}, u32[]{:S(2)}) collective-permute-start(bf16[16,3584]{1,0:T(8,128)(2,1)S(1)} %shard_map.97.refs_4_), channel_id=1, source_target_pairs={{0,3},{1,2},{2,1},{3,0},{4,7},{5,6},{6,5},{7,4},{8,11},{9,10},{10,... | collective-permute-start | bytes 344072 | tf_op jit(solution)/shard_map/ppermute | solution.py:219
  17.9 5.4 %collective-permute-start.8 = (bf16[16,3584]{1,0:T(8,128)(2,1)S(1)}, bf16[16,3584]{1,0:T(8,128)(2,1)S(1)}, u32[]{:S(2)}, u32[]{:S(2)}) collective-permute-start(bf16[16,3584]{1,0:T(8,128)(2,1)S(1)} %shard_map.97.refs_4_), channel_id=1, source_target_pairs={{0,2},{1,3},{2,0},{3,1},{4,5},{5,4},{6,7},{7,6},{8,10},{9,11},{10,... | collective-permute-start | bytes 344072 | tf_op jit(solution)/shard_map/ppermute | solution.py:228
  18.4 4.8 %collective-permute-start.7 = (bf16[16,3584]{1,0:T(8,128)(2,1)S(1)}, bf16[16,3584]{1,0:T(8,128)(2,1)S(1)}, u32[]{:S(2)}, u32[]{:S(2)}) collective-permute-start(bf16[16,3584]{1,0:T(8,128)(2,1)S(1)} %shard_map.97.refs_4_), channel_id=1, source_target_pairs={{0,1},{1,0},{2,3},{3,2},{4,6},{5,7},{6,4},{7,5},{8,9},{9,8},{10,11... | collective-permute-start | bytes 344072 | tf_op jit(solution)/shard_map/ppermute | solution.py:228

commit v6 on v5

--- a/solution.py
+++ b/solution.py
@@ -219,22 +219,11 @@
     return lax.ppermute(rows, axis, [(place, place ^ bits) for place in range(count)])
 
 
-def swap_by_core(rows, bits):
-    experts, count = lax.axis_size("expert"), lax.axis_size("dp")
-    pairs = []
-    for expert in range(experts):
-        for place in range(count):
-            pairs.append((expert * count + place, expert * count + (place ^ bits[expert % 2])))
-    return lax.ppermute(rows, ("expert", "dp"), pairs)
-
-
 def spread(rows):
     count = lax.axis_size("dp")
     if count > 4:
         return [lax.all_gather(rows, "dp", axis=0, tiled=True)]
-    if count < 4:
-        return [rows] + [swap(rows, "dp", bits) for bits in range(1, count)]
-    return [rows, swap_by_core(rows, (1, 2)), swap_by_core(rows, (2, 1)), swap(rows, "dp", 3)]
+    return [rows] + [swap(rows, "dp", bits) for bits in range(1, count)]
 
 
 def local(tokens, expert_ids, gate_probs, out_grad, w_gate, w_up, w_down):

time: 27.7 us -> 27.7 us (level)
    ppermute x4 -> x0, starting transfers between devices: 2.07 us -> none  [swap_by_core(): return lax.ppermute(rows, ('expert', 'dp'), pairs)]
    ppermute x3 -> x7, starting transfers between devices: 5.55 us -> 7.63 us  [swap(): lax.ppermute(rows, axis, [(place, place ^ bits) for place in range(count)])]
    ppermute x4 -> x0, waiting for transfers between devices: 1.19 us -> none  [swap_by_core(): return lax.ppermute(rows, ('expert', 'dp'), pairs)]
    ppermute x3 -> x7, waiting for transfers between devices: 1.47 us -> 2.66 us  [swap(): lax.ppermute(rows, axis, [(place, place ^ bits) for place in range(count)])]
where the time goes in v6:
time: 27.7 us; the launch traced here: 27.5 us
  starting transfers between devices  13.2 us (48%)
  Pallas kernels  8.75 us (32%)
  waiting for transfers between devices  4.91 us (18%)
  between operations  0.67 us (2%)
    ppermute x7, starting transfers between devices, swap(): lax.ppermute(rows, axis, [(place, place ^ bits) for place in range(count)])  7.63 us
    ppermute x3, starting transfers between devices, local(): arrived.append(lax.ppermute(block, 'expert', pairs) if place else block)  5.59 us
    pallas_call x1, Pallas kernels, weight_grads(): pl.pallas_call(functools.partial(grads_kernel, len(parts)), out_shape=(sh...  4.26 us
    ppermute x7, waiting for transfers between devices, swap(): lax.ppermute(rows, axis, [(place, place ^ bits) for place in range(count)])  2.66 us
    pallas_call x1, Pallas kernels, load_weights(): pl.pallas_call(load_kernel, out_shape=(shape, shape, shape), in_specs=[pl...  2.61 us
    ppermute x3, waiting for transfers between devices, local(): arrived.append(lax.ppermute(block, 'expert', pairs) if place else block)  2.25 us
    pallas_call x1, Pallas kernels, pick_rows(): pl.pallas_call(pick_kernel, out_shape=(shape, shape), in_specs=[HBM] * 4,...  1.82 us
  transfers between devices with their start and end apart: 10, of which 4 were waited for; matrix products, arithmetic and copies ran while one was open for 0% of the time, Pallas kernels for 10%

profile of v6, /device:TPU:0, one launch (start us, length us, event | category | flops | bytes accessed | tf_op | source)
XLA Modules:
  0.0 27.5 jit_solution(168796015547772502)
XLA Ops:
  0.6 1.8 %shard_map.94 = (bf16[16,3584]{1,0:T(8,128)(2,1)S(1)}, bf16[16,3584]{1,0:T(8,128)(2,1)S(1)}) custom-call(s32[8,128]{1,0:T(8,128)} %bitcast.11, f32[8,128]{1,0:T(8,128)} %bitcast.12, bf16[128,3584]{1,0:T(8,128)(2,1)} %tokens_hbm.1, bf16[128,3584]{1,0:T(8,128)(2,1)} %grad_hbm.1), custom_call_target="tpu_custom_call" | custom-call | tf_op jit(solution)/shard_map/pallas_call | solution.py:81
  2.5 0.5 %collective-permute-start = (bf16[16,3584]{1,0:T(8,128)(2,1)S(1)}, bf16[16,3584]{1,0:T(8,128)(2,1)S(1)}, u32[]{:S(2)}, u32[]{:S(2)}) collective-permute-start(bf16[16,3584]{1,0:T(8,128)(2,1)S(1)} %get-tuple-element.16), channel_id=1, source_target_pairs={{0,4},{4,0},{8,12},{12,8},{16,20},{20,16},{24,28},{28,24},{1,5},{5... | collective-permute-start | bytes 344072 | tf_op jit(solution)/shard_map/ppermute | solution.py:219
  3.0 1.0 %collective-permute-done.other_ref = bf16[16,3584]{1,0:T(8,128)(2,1)S(1)} collective-permute-done((bf16[16,3584]{1,0:T(8,128)(2,1)S(1)}, bf16[16,3584]{1,0:T(8,128)(2,1)S(1)}, u32[]{:S(2)}, u32[]{:S(2)}) %collective-permute-start) | collective-permute-done | bytes 114720 | tf_op jit(solution)/shard_map/ppermute | solution.py:219
  4.0 3.0 %collective-permute-start.1 = (bf16[8,3584]{1,0:T(8,128)(2,1)S(1)}, bf16[8,3584]{1,0:T(8,128)(2,1)S(1)}, u32[]{:S(2)}, u32[]{:S(2)}) collective-permute-start(bf16[8,3584]{1,0:T(8,128)(2,1)S(1)} %get-tuple-element.18), channel_id=1, source_target_pairs={{0,8},{4,12},{8,0},{12,4},{16,24},{20,28},{24,16},{28,20},{1,9},{5... | collective-permute-start | bytes 172040 | tf_op jit(solution)/shard_map/ppermute | solution.py:238
  7.0 2.5 %collective-permute-start.5 = (bf16[8,3584]{1,0:T(8,128)(2,1)S(1)}, bf16[8,3584]{1,0:T(8,128)(2,1)S(1)}, u32[]{:S(2)}, u32[]{:S(2)}) collective-permute-start(bf16[8,3584]{1,0:T(8,128)(2,1)S(1)} %get-tuple-element.19), channel_id=1, source_target_pairs={{0,24},{4,20},{8,16},{12,28},{16,8},{20,4},{24,0},{28,12},{1,25},{... | collective-permute-start | bytes 172040 | tf_op jit(solution)/shard_map/ppermute | solution.py:238
  9.5 0.1 collective-permute-start.6
  9.6 0.0 collective-permute-done.1.refs_0_
  9.6 2.5 %collective-permute-start.4 = (bf16[16,3584]{1,0:T(8,128)(2,1)S(1)}, bf16[16,3584]{1,0:T(8,128)(2,1)S(1)}, u32[]{:S(2)}, u32[]{:S(2)}) collective-permute-start(bf16[16,3584]{1,0:T(8,128)(2,1)S(1)} %shard_map.96.refs_1_.refs_0_), channel_id=1, source_target_pairs={{0,3},{1,2},{2,1},{3,0},{4,7},{5,6},{6,5},{7,4},{8,11},{9,10},{10,... | collective-permute-start | bytes 344072 | tf_op jit(solution)/shard_map/ppermute | solution.py:219
  12.1 0.5 %collective-permute-start.3 = (bf16[16,3584]{1,0:T(8,128)(2,1)S(1)}, bf16[16,3584]{1,0:T(8,128)(2,1)S(1)}, u32[]{:S(2)}, u32[]{:S(2)}) collective-permute-start(bf16[16,3584]{1,0:T(8,128)(2,1)S(1)} %shard_map.96.refs_1_.refs_0_), channel_id=1, source_target_pairs={{0,2},{1,3},{2,0},{3,1},{4,6},{5,7},{6,4},{7,5},{8,10},{9,11},{10,... | collective-permute-start | bytes 344072 | tf_op jit(solution)/shard_map/ppermute | solution.py:219
  12.6 0.5 %collective-permute-start.2 = (bf16[16,3584]{1,0:T(8,128)(2,1)S(1)}, bf16[16,3584]{1,0:T(8,128)(2,1)S(1)}, u32[]{:S(2)}, u32[]{:S(2)}) collective-permute-start(bf16[16,3584]{1,0:T(8,128)(2,1)S(1)} %shard_map.96.refs_1_.refs_0_), channel_id=1, source_target_pairs={{0,1},{1,0},{2,3},{3,2},{4,5},{5,4},{6,7},{7,6},{8,9},{9,8},{10,11... | collective-permute-start | bytes 344072 | tf_op jit(solution)/shard_map/ppermute | solution.py:219
  13.1 0.0 collective-permute-done.5.first_ref
  13.1 2.2 %collective-permute-done.6.refs_0_ = bf16[8,3584]{1,0:T(8,128)(2,1)S(1)} collective-permute-done((bf16[8,3584]{1,0:T(8,128)(2,1)S(1)}, bf16[8,3584]{1,0:T(8,128)(2,1)S(1)}, u32[]{:S(2)}, u32[]{:S(2)}) %collective-permute-start.6) | collective-permute-done | bytes 57376 | tf_op jit(solution)/shard_map/ppermute | solution.py:238
  15.4 2.5 %collective-permute-start.9 = (bf16[16,3584]{1,0:T(8,128)(2,1)S(1)}, bf16[16,3584]{1,0:T(8,128)(2,1)S(1)}, u32[]{:S(2)}, u32[]{:S(2)}) collective-permute-start(bf16[16,3584]{1,0:T(8,128)(2,1)S(1)} %shard_map.97.refs_4_), channel_id=1, source_target_pairs={{0,3},{1,2},{2,1},{3,0},{4,7},{5,6},{6,5},{7,4},{8,11},{9,10},{10,... | collective-permute-start | bytes 344072 | tf_op jit(solution)/shard_map/ppermute | solution.py:219
  17.9 0.5 %collective-permute-start.8 = (bf16[16,3584]{1,0:T(8,128)(2,1)S(1)}, bf16[16,3584]{1,0:T(8,128)(2,1)S(1)}, u32[]{:S(2)}, u32[]{:S(2)}) collective-permute-start(bf16[16,3584]{1,0:T(8,128)(2,1)S(1)} %shard_map.97.refs_4_), channel_id=1, source_target_pairs={{0,2},{1,3},{2,0},{3,1},{4,6},{5,7},{6,4},{7,5},{8,10},{9,11},{10,... | collective-permute-start | bytes 344072 | tf_op jit(solution)/shard_map/ppermute | solution.py:219
  18.4 0.0 collective-permute-done.4.refs_3_
  18.4 0.5 %collective-permute-start.7 = (bf16[16,3584]{1,0:T(8,128)(2,1)S(1)}, bf16[16,3584]{1,0:T(8,128)(2,1)S(1)}, u32[]{:S(2)}, u32[]{:S(2)}) collective-permute-start(bf16[16,3584]{1,0:T(8,128)(2,1)S(1)} %shard_map.97.refs_4_), channel_id=1, source_target_pairs={{0,1},{1,0},{2,3},{3,2},{4,5},{5,4},{6,7},{7,6},{8,9},{9,8},{10,11... | collective-permute-start | bytes 344072 | tf_op jit(solution)/shard_map/ppermute | solution.py:219
  19.0 0.0 collective-permute-done.3.refs_2_
  19.0 0.0 collective-permute-done.2.refs_1_
  19.0 2.6 %shard_map.98 = (bf16[256,3584]{1,0:T(8,128)(2,1)S(1)}, bf16[256,3584]{1,0:T(8,128)(2,1)S(1)}, bf16[256,3584]{1,0:T(8,128)(2,1)S(1)}) custom-call(bf16[16,3584]{1,0:T(8,128)(2,1)S(1)} %shard_map.96.refs_1_.refs_0_, bf16[16,3584]{1,0:T(8,128)(2,1)S(1)} %collective-permute-done.2.refs_1_, bf16[16,3584]{1,0:T(8,128)(2,1)S(1)} %collective-permute-done.3.refs_2_, ...), custom_call_target="tpu_custom_call" | custom-call | bytes 11010048 | tf_op jit(solution)/shard_map/pallas_call | solution.py:113
  21.6 0.5 %collective-permute-done.9.refs_7_ = bf16[16,3584]{1,0:T(8,128)(2,1)S(1)} collective-permute-done((bf16[16,3584]{1,0:T(8,128)(2,1)S(1)}, bf16[16,3584]{1,0:T(8,128)(2,1)S(1)}, u32[]{:S(2)}, u32[]{:S(2)}) %collective-permute-start.9) | collective-permute-done | bytes 114720 | tf_op jit(solution)/shard_map/ppermute | solution.py:219
  22.1 1.2 %collective-permute-done.8.refs_6_ = bf16[16,3584]{1,0:T(8,128)(2,1)S(1)} collective-permute-done((bf16[16,3584]{1,0:T(8,128)(2,1)S(1)}, bf16[16,3584]{1,0:T(8,128)(2,1)S(1)}, u32[]{:S(2)}, u32[]{:S(2)}) %collective-permute-start.8) | collective-permute-done | bytes 114720 | tf_op jit(solution)/shard_map/ppermute | solution.py:219
  23.3 0.0 collective-permute-done.7.refs_5_
  23.3 4.3 %shard_map.99 = (bf16[256,3584]{1,0:T(8,128)(2,1)}, bf16[256,3584]{1,0:T(8,128)(2,1)}, bf16[256,3584]{1,0:T(8,128)(2,1)}) custom-call(bf16[16,3584]{1,0:T(8,128)(2,1)S(1)} %shard_map.96.refs_1_.refs_0_, bf16[16,3584]{1,0:T(8,128)(2,1)S(1)} %collective-permute-done.2.refs_1_, bf16[16,3584]{1,0:T(8,128)(2,1)S(1)} %collective-permute-done.3.refs_2_, ...), custom_call_target="tpu_custom_call" | custom-call | tf_op jit(solution)/shard_map/pallas_call | solution.py:203
  (3 shorter events, 0.1 us)
Async XLA Ops:
  2.5 1.5 %collective-permute-start = (bf16[16,3584]{1,0:T(8,128)(2,1)S(1)}, bf16[16,3584]{1,0:T(8,128)(2,1)S(1)}, u32[]{:S(2)}, u32[]{:S(2)}) collective-permute-start(bf16[16,3584]{1,0:T(8,128)(2,1)S(1)} %get-tuple-element.16), channel_id=1, source_target_pairs={{0,4},{4,0},{8,12},{12,8},{16,20},{20,16},{24,28},{28,24},{1,5},{5... | collective-permute-start | bytes 344072 | tf_op jit(solution)/shard_map/ppermute | solution.py:219
  4.0 5.6 %collective-permute-start.1 = (bf16[8,3584]{1,0:T(8,128)(2,1)S(1)}, bf16[8,3584]{1,0:T(8,128)(2,1)S(1)}, u32[]{:S(2)}, u32[]{:S(2)}) collective-permute-start(bf16[8,3584]{1,0:T(8,128)(2,1)S(1)} %get-tuple-element.18), channel_id=1, source_target_pairs={{0,8},{4,12},{8,0},{12,4},{16,24},{20,28},{24,16},{28,20},{1,9},{5... | collective-permute-start | bytes 172040 | tf_op jit(solution)/shard_map/ppermute | solution.py:238
  7.0 6.2 %collective-permute-start.5 = (bf16[8,3584]{1,0:T(8,128)(2,1)S(1)}, bf16[8,3584]{1,0:T(8,128)(2,1)S(1)}, u32[]{:S(2)}, u32[]{:S(2)}) collective-permute-start(bf16[8,3584]{1,0:T(8,128)(2,1)S(1)} %get-tuple-element.19), channel_id=1, source_target_pairs={{0,24},{4,20},{8,16},{12,28},{16,8},{20,4},{24,0},{28,12},{1,25},{... | collective-permute-start | bytes 172040 | tf_op jit(solution)/shard_map/ppermute | solution.py:238
  9.5 5.9 %collective-permute-start.6 = (bf16[8,3584]{1,0:T(8,128)(2,1)S(1)}, bf16[8,3584]{1,0:T(8,128)(2,1)S(1)}, u32[]{:S(2)}, u32[]{:S(2)}) collective-permute-start(bf16[8,3584]{1,0:T(8,128)(2,1)S(1)} %get-tuple-element.20), channel_id=1, source_target_pairs={{0,16},{4,28},{8,24},{12,20},{16,0},{20,12},{24,8},{28,4},{1,17},{... | collective-permute-start | bytes 172040 | tf_op jit(solution)/shard_map/ppermute | solution.py:238
  9.6 8.8 %collective-permute-start.4 = (bf16[16,3584]{1,0:T(8,128)(2,1)S(1)}, bf16[16,3584]{1,0:T(8,128)(2,1)S(1)}, u32[]{:S(2)}, u32[]{:S(2)}) collective-permute-start(bf16[16,3584]{1,0:T(8,128)(2,1)S(1)} %shard_map.96.refs_1_.refs_0_), channel_id=1, source_target_pairs={{0,3},{1,2},{2,1},{3,0},{4,7},{5,6},{6,5},{7,4},{8,11},{9,10},{10,... | collective-permute-start | bytes 344072 | tf_op jit(solution)/shard_map/ppermute | solution.py:219
  12.1 6.9 %collective-permute-start.3 = (bf16[16,3584]{1,0:T(8,128)(2,1)S(1)}, bf16[16,3584]{1,0:T(8,128)(2,1)S(1)}, u32[]{:S(2)}, u32[]{:S(2)}) collective-permute-start(bf16[16,3584]{1,0:T(8,128)(2,1)S(1)} %shard_map.96.refs_1_.refs_0_), channel_id=1, source_target_pairs={{0,2},{1,3},{2,0},{3,1},{4,6},{5,7},{6,4},{7,5},{8,10},{9,11},{10,... | collective-permute-start | bytes 344072 | tf_op jit(solution)/shard_map/ppermute | solution.py:219
  12.6 6.4 %collective-permute-start.2 = (bf16[16,3584]{1,0:T(8,128)(2,1)S(1)}, bf16[16,3584]{1,0:T(8,128)(2,1)S(1)}, u32[]{:S(2)}, u32[]{:S(2)}) collective-permute-start(bf16[16,3584]{1,0:T(8,128)(2,1)S(1)} %shard_map.96.refs_1_.refs_0_), channel_id=1, source_target_pairs={{0,1},{1,0},{2,3},{3,2},{4,5},{5,4},{6,7},{7,6},{8,9},{9,8},{10,11... | collective-permute-start | bytes 344072 | tf_op jit(solution)/shard_map/ppermute | solution.py:219
  15.4 6.6 %collective-permute-start.9 = (bf16[16,3584]{1,0:T(8,128)(2,1)S(1)}, bf16[16,3584]{1,0:T(8,128)(2,1)S(1)}, u32[]{:S(2)}, u32[]{:S(2)}) collective-permute-start(bf16[16,3584]{1,0:T(8,128)(2,1)S(1)} %shard_map.97.refs_4_), channel_id=1, source_target_pairs={{0,3},{1,2},{2,1},{3,0},{4,7},{5,6},{6,5},{7,4},{8,11},{9,10},{10,... | collective-permute-start | bytes 344072 | tf_op jit(solution)/shard_map/ppermute | solution.py:219
  17.9 5.4 %collective-permute-start.8 = (bf16[16,3584]{1,0:T(8,128)(2,1)S(1)}, bf16[16,3584]{1,0:T(8,128)(2,1)S(1)}, u32[]{:S(2)}, u32[]{:S(2)}) collective-permute-start(bf16[16,3584]{1,0:T(8,128)(2,1)S(1)} %shard_map.97.refs_4_), channel_id=1, source_target_pairs={{0,2},{1,3},{2,0},{3,1},{4,6},{5,7},{6,4},{7,5},{8,10},{9,11},{10,... | collective-permute-start | bytes 344072 | tf_op jit(solution)/shard_map/ppermute | solution.py:219
  18.4 4.8 %collective-permute-start.7 = (bf16[16,3584]{1,0:T(8,128)(2,1)S(1)}, bf16[16,3584]{1,0:T(8,128)(2,1)S(1)}, u32[]{:S(2)}, u32[]{:S(2)}) collective-permute-start(bf16[16,3584]{1,0:T(8,128)(2,1)S(1)} %shard_map.97.refs_4_), channel_id=1, source_target_pairs={{0,1},{1,0},{2,3},{3,2},{4,5},{5,4},{6,7},{7,6},{8,9},{9,8},{10,11... | collective-permute-start | bytes 344072 | tf_op jit(solution)/shard_map/ppermute | solution.py:219
